TPU v7x, 32 devices: a whole 2x2x4 slice. The times are simulated.
32 devices in a mesh: row: 4 (over y, core), col: 8 (over z, x).
Axes of the slice: x: 2, y: 2, z: 4, core: 2. Of those that a mesh axis runs over, the one named last changes fastest.
Arguments:
- weights: float32 [40, 2048, 4096], P(None, 'row', 'col'), may hold values from -0.006214806 to 0.006214806
- pool: float32 [12, 2048, 4096], P(None, 'row', 'col'), may hold values from -6 to 6
- desired: float32 [12, 8], replicated, may hold values from -6 to 6
- plan: int32 [2, 16], replicated, may hold values from 0 to 11
- beam_ref: int32 [40], replicated, may hold values from 0 to 7
- step_size: float32 [40], replicated, may hold values from 0.2 to 0.8
- smoothing: float32 [40], replicated, may hold values from 0.05 to 0.2
- active: int32 [40], replicated, may hold values from 1 to 2
Outputs:
- final_weights: float32 [40, 2048, 4096], P(None, 'row', 'col')
- errors: float32 [2, 40, 16], replicated
Inputs may be any that keep to these rules, and one draw needn't show every extreme that they name: `plan`: indices of recorded snapshots. `beam_ref`: indices of reference signals.
All inputs are finite; a program needn't handle non-finite values.
Results may differ from a plain program's by a relative error of at most 0.00017.
Values sent between devices are 32-bit elements; how exact they have to be, the bound alone decides.
A program may use at most 384 MiB of HBM per device.

v0:
```python
import math

import jax
import jax.numpy as jnp
from jax import lax
from jax.sharding import PartitionSpec as P

NR = 2048
NC = 4096
ITERS = 2


def padded_2(value, sides, width):
    for axis, dim in sides:
        count, length = (lax.axis_size(axis), value.shape[dim])
        up = [(i, (i + 1) % count) for i in range(count - 1)]
        down = [(j, i) for i, j in up]
        last = lax.slice_in_dim(value, length - width, length, axis=dim)
        leading = lax.slice_in_dim(value, 0, width, axis=dim)
        before = lax.ppermute(last, axis, up)
        after = lax.ppermute(leading, axis, down)
        value = jnp.concatenate([before, value, after], axis=dim)
    return value


def stencil(padded):
    center = padded[:, 1:-1, 1:-1]
    return (
        padded[:, 2:, 1:-1]
        + padded[:, :-2, 1:-1]
        + padded[:, 1:-1, 2:]
        + padded[:, 1:-1, :-2]
        - 4.0 * center
    )


def beam_sum(inner, snaps, scale):
    local = jnp.dot(
        inner.reshape(inner.shape[0], -1),
        snaps.reshape(snaps.shape[0], -1).T,
        precision=lax.Precision.HIGHEST,
    )
    return lax.psum(local, ("row", "col")) * scale


def body(weights, pool, desired, plan, beam_ref, step_size, smoothing, active):
    count = pool.shape[0]
    scale = 1.0 / math.sqrt(NR * NC)
    refs = desired.shape[1]
    pick = (beam_ref[:, None] == jnp.arange(refs, dtype=jnp.int32)[None, :]).astype(jnp.float32)
    targets = jnp.dot(pick, desired.T, precision=lax.Precision.HIGHEST)
    rate = (step_size * scale)[:, None, None]
    smooth = smoothing[:, None, None]
    history = []
    current = weights
    for step in range(ITERS):
        snaps = jnp.take(pool, plan[step], axis=0)
        beam_out = beam_sum(current, snaps, scale)
        padded = padded_2(current, (("row", 1), ("col", 2)), 1)
        lap = stencil(padded)
        select = (plan[step][None, :] == jnp.arange(count, dtype=jnp.int32)[:, None]).astype(
            jnp.float32
        )
        error = jnp.dot(targets, select, precision=lax.Precision.HIGHEST) - beam_out
        history.append(error)
        grad = jnp.dot(
            error, snaps.reshape(snaps.shape[0], -1), precision=lax.Precision.HIGHEST
        ).reshape(current.shape)
        live = (active > step).astype(jnp.float32)[:, None, None]
        current = current + live * (rate * grad + smooth * lap)
    return (current, jnp.stack(history))


def solution(mesh):
    in_specs = (P(None, "row", "col"), P(None, "row", "col"), P(), P(), P(), P(), P(), P())
    out_specs = (P(None, "row", "col"), P())
    return jax.shard_map(body, mesh=mesh, in_specs=in_specs, out_specs=out_specs, check_vma=False)
```

profile of v0, /device:TPU:1, one launch (start us, length us, event | category | flops | bytes accessed | tf_op | source)
XLA Modules:
  0.0 718.8 jit_solution(5819591964200601075)
XLA Ops:
  0.6 0.0 copy-start
  0.6 0.0 copy-start.2
  0.7 38.9 %copy.47 = f32[40,512,512]{2,0,1:T(8,128)} copy(f32[40,512,512]{2,1,0:T(8,128)} %param.10) | data formatting | bytes 83886080 | tf_op args[0]
  39.5 0.9 fusion.39
  40.5 4.5 collective-permute-start.1
  45.0 2.1 collective-permute-start
  47.1 0.0 copy-done.2
  47.2 0.5 slice_bitcast_fusion
  47.7 12.7 %gather_fusion = f32[16,512,512]{2,1,0:T(8,128)} fusion(f32[12,512,512]{2,1,0:T(8,128)} %param.11, s32[1024]{0:T(1024)S(1)} %pad_clamp_fusion.1), kind=kCustom, calls=%fused_computation.clone | custom fusion | bytes 33554496 | tf_op jit(solution)/shard_map/jit(_take)/gather | solution.py:57
  60.4 12.0 %broadcast_select_fusion.1 = f32[16,512,512]{2,1,0:T(8,128)} fusion(f32[16,512,512]{2,1,0:T(8,128)} %gather_fusion, pred[16]{0:T(512)(128)(4,1)S(1)} %get-tuple-element.23), kind=kLoop, calls=%fused_computation.42 | loop fusion | flops 4194304 | bytes 33554448 | tf_op jit(solution)/shard_map/jit(_take)/select_n | solution.py:57
  72.4 0.0 copy-start.4
  72.4 73.3 %fusion.24 = f32[40,16]{0,1:T(8,128)S(1)} fusion(f32[16,512,512]{2,1,0:T(8,128)} %broadcast_select_fusion.1, f32[40,512,512]{2,1,0:T(8,128)} %param.10), kind=kOutput, calls=%fused_computation.43 | convolution fusion | flops 2013265920 | bytes 58722816 | tf_op jit(solution)/shard_map/dot_general | solution.py:38
  145.7 0.0 copy-start.5
  145.7 40.0 %psum.14 = f32[40,16]{0,1:T(8,128)S(1)} all-reduce(f32[40,16]{0,1:T(8,128)S(1)} %fusion.24), channel_id=1, replica_groups=mesh['row'=4,'col'=8] {'row','col'}, use_global_device_ids=true, to_apply=%region_0.0 | all-reduce | flops 640 | bytes 5120 | tf_op jit(solution)/shard_map/psum | solution.py:43
  185.7 12.7 %gather_fusion.1 = f32[16,512,512]{2,1,0:T(8,128)} fusion(f32[12,512,512]{2,1,0:T(8,128)} %param.11, s32[1024]{0:T(1024)S(1)} %pad_clamp_fusion), kind=kCustom, calls=%fused_computation.1.clone | custom fusion | bytes 33554496 | tf_op jit(solution)/shard_map/jit(_take)/gather | solution.py:57
  198.4 0.0 copy-done
  198.4 0.0 copy-done.4
  198.4 0.2 fusion.30
  198.6 11.9 %broadcast_select_fusion = f32[16,512,512]{2,1,0:T(8,128)} fusion(f32[16,512,512]{2,1,0:T(8,128)} %gather_fusion.1, pred[16]{0:T(512)(128)(4,1)S(1)} %get-tuple-element.9), kind=kLoop, calls=%fused_computation.41 | loop fusion | flops 4194304 | bytes 33554448 | tf_op jit(solution)/shard_map/jit(_take)/select_n | solution.py:57
  210.5 0.2 convolution_subtract_fusion.1
  210.7 0.0 copy-done.5
  210.7 0.5 compare_convert_fusion
  211.2 0.0 collective-permute-done.1
  211.2 0.7 constant_dynamic-update-slice_fusion.2
  211.8 38.9 %constant_dynamic-update-slice_fusion.1 = f32[40,514,512]{2,0,1:T(8,128)} fusion(f32[40,514,512]{2,0,1:T(8,128)} %constant_dynamic-update-slice_fusion.2, f32[40,512,512]{2,1,0:T(8,128)} %param.10), kind=kLoop, calls=%fused_computation.56 | loop fusion | bytes 83886080
  250.7 0.0 copy-start.6
  250.7 0.0 collective-permute-done
  250.8 0.6 constant_dynamic-update-slice_fusion
  251.4 0.0 copy-start.7
  251.4 16.2 %fusion.37 = (f32[40,514,1]{2,0,1:T(8,128)}, f32[40,514,1]{2,0,1:T(8,128)}) fusion(f32[40,514,512]{2,0,1:T(8,128)} %constant_dynamic-update-slice_fusion), kind=kLoop, calls=%fused_computation.72 | loop fusion | bytes 328960 | tf_op jit(solution)/shard_map/slice | solution.py:19
  267.6 7.2 copy.42
  274.8 1.3 collective-permute-start.2
  276.1 7.2 %copy.44 = f32[40,514,1]{1,0,2:T(8,128)S(1)} copy(f32[40,514,1]{2,0,1:T(8,128)} %get-tuple-element.16) | data formatting | bytes 164480 | tf_op jit(solution)/shard_map/slice | solution.py:18
  283.3 4.4 collective-permute-start.3
  287.7 0.0 copy-done.6
  287.7 0.0 collective-permute-done.2
  287.7 6.6 copy.43
  294.4 0.0 collective-permute-done.3
  294.4 6.8 copy.45
  301.2 0.0 copy-done.7
  301.2 114.0 %fusion.13 = f32[40,512,512]{2,0,1:T(8,128)} fusion(f32[40,512,512]{2,0,1:T(8,128)} %copy.47, f32[40,514,512]{2,0,1:T(8,128)} %constant_dynamic-update-slice_fusion, f32[40,514,1]{2,0,1:T(8,128)} %copy.45, f32[40,514,1]{2,0,1:T(8,128)} %copy.43, f32[40,1,512]{2,0,1:T(8,128)S(1)} %collective-permute-done.1, f32[40,1,512]{2,0,1:T(8,128)S(1)} %collective-permute-done, ...), kind=kOutput, calls=%fused_computation.24 | convolution fusion | flops 2160066560 | bytes 143101536 | tf_op jit(solution)/shard_map/dot_general | solution.py:66
  415.2 1.0 fusion.38
  416.1 4.2 collective-permute-start.4
  420.3 3.7 collective-permute-start.5
  424.1 41.0 %fusion.27 = f32[40,16]{0,1:T(8,128)S(1)} fusion(f32[40,512,512]{2,0,1:T(8,128)} %fusion.13, f32[16,512,512]{2,1,0:T(8,128)} %broadcast_select_fusion), kind=kOutput, calls=%fused_computation.44 | convolution fusion | flops 2013265920 | bytes 58722816 | tf_op jit(solution)/shard_map/dot_general | solution.py:38
  465.1 38.2 %psum.15 = f32[40,16]{0,1:T(8,128)S(1)} all-reduce(f32[40,16]{0,1:T(8,128)S(1)} %fusion.27), channel_id=1, replica_groups=mesh['row'=4,'col'=8] {'row','col'}, use_global_device_ids=true, to_apply=%region_1.3 | all-reduce | flops 640 | bytes 5120 | tf_op jit(solution)/shard_map/psum | solution.py:43
  503.3 0.0 copy-done.3
  503.3 0.2 convolution_subtract_fusion
  503.5 0.0 collective-permute-done.4
  503.5 0.0 collective-permute-done.5
  503.5 17.8 %pad_maximum_fusion.14 = (f32[40,514,1]{2,0,1:T(8,128)}, f32[40,514,1]{2,0,1:T(8,128)}) fusion(f32[40,1,512]{2,0,1:T(8,128)S(1)} %collective-permute-done.4, f32[40,512,512]{2,0,1:T(8,128)} %fusion.13, f32[40,1,512]{2,0,1:T(8,128)S(1)} %collective-permute-done.5), kind=kLoop, calls=%fused_computation.40 | loop fusion | flops 82240 | bytes 42271360 | tf_op jit(solution)/shard_map/slice | solution.py:19
  521.4 7.2 copy.50
  528.5 1.3 collective-permute-start.6
  529.8 7.2 copy.52
  537.0 4.7 collective-permute-start.7
  541.7 0.6 pad_maximum_fusion.15
  542.3 0.0 collective-permute-done.6
  542.3 6.9 copy.51
  549.2 0.0 collective-permute-done.7
  549.2 6.4 copy.53
  555.5 0.0 copy-done.8
  555.5 124.2 %fusion.5 = f32[40,512,512]{2,0,1:T(8,128)} fusion(f32[40,512,512]{2,0,1:T(8,128)} %fusion.13, f32[40,514,1]{2,0,1:T(8,128)} %copy.53, f32[40,1,512]{2,0,1:T(8,128)S(1)} %collective-permute-done.4, f32[40,1,512]{2,0,1:T(8,128)S(1)} %collective-permute-done.5, f32[40,514,1]{2,0,1:T(8,128)} %copy.51, f32[40]{0:T(128)S(1)} %copy-done.8, f32[40]{0:T(128)S(1)} %copy-done.7, ...), kind=kOutput, calls=%fused_computation.8 | convolution fusion | flops 2202009600 | bytes 100994656 | tf_op jit(solution)/shard_map/dot_general | solution.py:66
  679.7 38.8 %copy.54 = f32[40,512,512]{2,1,0:T(8,128)} copy(f32[40,512,512]{2,0,1:T(8,128)} %fusion.5) | data formatting | bytes 83886080
  718.6 0.0 copy-done.1
  (7 shorter events, 0.0 us)
Async XLA Ops:
  0.6 197.7 %copy-start = (f32[12,8]{0,1:T(8,128)S(1)}, f32[12,8]{0,1:T(8,128)}, u32[]{:S(2)}) copy-start(f32[12,8]{0,1:T(8,128)} %param.12) | copy-start | bytes 1156
  0.6 46.5 %copy-start.2 = (s32[2,16]{1,0:T(2,128)S(1)}, s32[2,16]{1,0:T(2,128)}, u32[]{:S(2)}) copy-start(s32[2,16]{1,0:T(2,128)} %param.13) | copy-start | bytes 388
  40.5 170.7 %collective-permute-start.1 = (f32[40,1,512]{2,0,1:T(8,128)S(1)}, f32[40,1,512]{2,0,1:T(8,128)S(1)}, u32[]{:S(2)}, u32[]{:S(2)}) collective-permute-start(f32[40,1,512]{2,0,1:T(8,128)S(1)} %get-tuple-element.20), channel_id=1, source_target_pairs={{0,8},{8,16},{16,24},{1,9},{9,17},{17,25},{2,10},{10,18},{18,26},{... | collective-permute-start | bytes 245768 | tf_op jit(solution)/shard_map/ppermute | solution.py:20
  45.0 205.7 %collective-permute-start = (f32[40,1,512]{2,0,1:T(8,128)S(1)}, f32[40,1,512]{2,0,1:T(8,128)S(1)}, u32[]{:S(2)}, u32[]{:S(2)}) collective-permute-start(f32[40,1,512]{2,0,1:T(8,128)S(1)} %get-tuple-element.19), channel_id=1, source_target_pairs={{8,0},{16,8},{24,16},{9,1},{17,9},{25,17},{10,2},{18,10},{26,18},{... | collective-permute-start | bytes 245768 | tf_op jit(solution)/shard_map/ppermute | solution.py:21
  72.4 126.0 %copy-start.4 = (s32[40]{0:T(128)S(1)}, s32[40]{0:T(128)}, u32[]{:S(2)}) copy-start(s32[40]{0:T(128)} %param.14) | copy-start | bytes 484
  145.7 65.0 %copy-start.5 = (s32[40]{0:T(128)S(1)}, s32[40]{0:T(128)}, u32[]{:S(2)}) copy-start(s32[40]{0:T(128)} %param.17) | copy-start | bytes 484
  250.7 37.0 %copy-start.6 = (f32[40]{0:T(128)S(1)}, f32[40]{0:T(128)}, u32[]{:S(2)}) copy-start(f32[40]{0:T(128)} %param.15) | copy-start | bytes 484
  251.4 49.8 %copy-start.7 = (f32[40]{0:T(128)S(1)}, f32[40]{0:T(128)}, u32[]{:S(2)}) copy-start(f32[40]{0:T(128)} %param.16) | copy-start | bytes 484
  274.8 13.0 %collective-permute-start.2 = (f32[40,514,1]{1,0,2:T(8,128)S(1)}, f32[40,514,1]{1,0,2:T(8,128)S(1)}, u32[]{:S(2)}, u32[]{:S(2)}) collective-permute-start(f32[40,514,1]{1,0,2:T(8,128)S(1)} %copy.42), channel_id=1, source_target_pairs={{1,0},{2,1},{3,2},{4,3},{5,4},{6,5},{7,6},{9,8},{10,9},{11,10},{12... | collective-permute-start | bytes 246728 | tf_op jit(solution)/shard_map/ppermute | solution.py:21
  283.3 11.1 %collective-permute-start.3 = (f32[40,514,1]{1,0,2:T(8,128)S(1)}, f32[40,514,1]{1,0,2:T(8,128)S(1)}, u32[]{:S(2)}, u32[]{:S(2)}) collective-permute-start(f32[40,514,1]{1,0,2:T(8,128)S(1)} %copy.44), channel_id=1, source_target_pairs={{0,1},{1,2},{2,3},{3,4},{4,5},{5,6},{6,7},{8,9},{9,10},{10,11},{11... | collective-permute-start | bytes 246728 | tf_op jit(solution)/shard_map/ppermute | solution.py:20
  415.2 88.2 %copy-start.3 = (s32[16]{0:T(128)S(1)}, s32[16]{0:T(128)}, u32[]{:S(2)}) copy-start(s32[16]{0:T(128)} %get-tuple-element.21) | copy-start | bytes 196
  416.1 87.4 %collective-permute-start.4 = (f32[40,1,512]{2,0,1:T(8,128)S(1)}, f32[40,1,512]{2,0,1:T(8,128)S(1)}, u32[]{:S(2)}, u32[]{:S(2)}) collective-permute-start(f32[40,1,512]{2,0,1:T(8,128)S(1)} %get-tuple-element.18), channel_id=1, source_target_pairs={{8,0},{16,8},{24,16},{9,1},{17,9},{25,17},{10,2},{18,10},{26,18},{... | collective-permute-start | bytes 245768 | tf_op jit(solution)/shard_map/ppermute | solution.py:21
  420.3 83.2 %collective-permute-start.5 = (f32[40,1,512]{2,0,1:T(8,128)S(1)}, f32[40,1,512]{2,0,1:T(8,128)S(1)}, u32[]{:S(2)}, u32[]{:S(2)}) collective-permute-start(f32[40,1,512]{2,0,1:T(8,128)S(1)} %get-tuple-element.17), channel_id=1, source_target_pairs={{0,8},{8,16},{16,24},{1,9},{9,17},{17,25},{2,10},{10,18},{18,26},{... | collective-permute-start | bytes 245768 | tf_op jit(solution)/shard_map/ppermute | solution.py:20
  503.5 52.0 %copy-start.8 = (f32[40]{0:T(128)S(1)}, f32[40]{0:T(128)}, u32[]{:S(2)}) copy-start(f32[40]{0:T(128)} %get-tuple-element.25) | copy-start | bytes 484
  528.5 13.8 %collective-permute-start.6 = (f32[40,514,1]{1,0,2:T(8,128)S(1)}, f32[40,514,1]{1,0,2:T(8,128)S(1)}, u32[]{:S(2)}, u32[]{:S(2)}) collective-permute-start(f32[40,514,1]{1,0,2:T(8,128)S(1)} %copy.50), channel_id=1, source_target_pairs={{1,0},{2,1},{3,2},{4,3},{5,4},{6,5},{7,6},{9,8},{10,9},{11,10},{12... | collective-permute-start | bytes 246728 | tf_op jit(solution)/shard_map/ppermute | solution.py:21
  537.0 12.2 %collective-permute-start.7 = (f32[40,514,1]{1,0,2:T(8,128)S(1)}, f32[40,514,1]{1,0,2:T(8,128)S(1)}, u32[]{:S(2)}, u32[]{:S(2)}) collective-permute-start(f32[40,514,1]{1,0,2:T(8,128)S(1)} %copy.52), channel_id=1, source_target_pairs={{0,1},{1,2},{2,3},{3,4},{4,5},{5,6},{6,7},{8,9},{9,10},{10,11},{11... | collective-permute-start | bytes 246728 | tf_op jit(solution)/shard_map/ppermute | solution.py:20
  555.5 163.0 %copy-start.1 = (f32[12,8]{0,1:T(8,128)S(1)}, f32[12,8]{0,1:T(8,128)}, u32[]{:S(2)}) copy-start(f32[12,8]{0,1:T(8,128)} %param.12) | copy-start | bytes 1156
where the time goes:
time: 725 us; the launch traced here: 719 us
  matrix products  353 us (49%)
  local copies, waits for them, and re-layouts  217 us (30%)
  blocking collectives  78.2 us (11%)
  other arithmetic  42.9 us (6%)
  starting transfers between devices  26.3 us (4%)
    dot_general x2, matrix products, body(): jnp.dot(error, snaps.reshape(snaps.shape[0], -1), precision=lax.Precision...  238 us
    unnamed x22, local copies, waits for them, and re-layouts  117 us
    dot_general x2, matrix products, beam_sum(): jnp.dot(inner.reshape(inner.shape[0], -1), snaps.reshape(snaps.shape[0],...  114 us
    psum x2, blocking collectives, beam_sum(): return lax.psum(local, ('row', 'col')) * scale  78.2 us
    slice x4, local copies, waits for them, and re-layouts, padded_2(): leading = lax.slice_in_dim(value, 0, width, axis=dim)  31.5 us
    gather x2, local copies, waits for them, and re-layouts, body(): snaps = jnp.take(pool, plan[step], axis=0)  25.4 us
    select_n x2, other arithmetic, body(): snaps = jnp.take(pool, plan[step], axis=0)  23.9 us
    slice x1, other arithmetic, padded_2(): leading = lax.slice_in_dim(value, 0, width, axis=dim)  17.8 us
  transfers between devices with their start and end apart: 8, of which 0 were waited for; matrix products, arithmetic and copies ran while one was open for 32% of the time, Pallas kernels for 0%

commit v1 on v0

v1 whole, which is shorter than its diff:
```python
import functools
import math

import jax
import jax.numpy as jnp
from jax import lax
from jax.experimental import pallas as pl
from jax.experimental.pallas import tpu as pltpu
from jax.sharding import PartitionSpec as P

F32 = jnp.float32
BF16 = jnp.bfloat16
NT = (((1,), (1,)), ((), ()))
LIMIT = 56 * 1024 * 1024


def split(x):
    hi = x.astype(BF16)
    lo = (x - hi.astype(F32)).astype(BF16)
    return hi, lo


def neighbours(x, axis):
    size = x.shape[axis]
    return pltpu.roll(x, 1, axis) + pltpu.roll(x, size - 1, axis)


def laplacian(x):
    return neighbours(x, 0) + neighbours(x, 1) - 4.0 * x


def one_hot(rows, cols, hit):
    r = lax.broadcasted_iota(jnp.int32, (rows, cols), 0)
    c = lax.broadcasted_iota(jnp.int32, (rows, cols), 1)
    return jnp.where(hit(r, c), 1.0, 0.0).astype(F32)


def moments_kernel(w_ref, x_ref, xp_ref, xn_ref, xt_ref, xb_ref, xe_ref, out_ref, lx_ref, el_ref, er_ref, acc_ref):
    i, last = pl.program_id(0), pl.num_programs(0) - 1
    beams, rows, cols = w_ref.shape
    pool = x_ref.shape[0]

    @pl.when(i == 0)
    def _():
        acc_ref[...] = jnp.zeros_like(acc_ref)

    for p in range(pool):
        above = jnp.where(i == 0, xt_ref[p], xp_ref[p])
        below = jnp.where(i == last, xb_ref[p], xn_ref[p])
        cur = x_ref[p]
        tall = jnp.concatenate([above, cur, below], axis=0)
        wide = jnp.concatenate([cur, xe_ref[p]], axis=1)
        lx_ref[p] = neighbours(tall, 0)[8 : rows + 8] + neighbours(wide, 1)[:, :cols] - 4.0 * cur

    for g in range(rows // 8):
        part = pl.ds(8 * g, 8)
        wg = w_ref[:, part, :].reshape(beams * 8, cols)
        xg = x_ref[:, part, :].reshape(pool * 8, cols)
        lg = lx_ref[:, part, :].reshape(pool * 8, cols)
        lh, ll = split(jnp.concatenate([wg, xg], axis=0))
        rh, rl = split(jnp.concatenate([xg, lg], axis=0))
        left = jnp.concatenate([lh, ll, lh], axis=1)
        right = jnp.concatenate([rh, rh, rl], axis=1)
        acc_ref[...] += lax.dot_general(left, right, NT, preferred_element_type=F32)

    def edge(tile, lane):
        pick = one_hot(8, 128, lambda r, c: c == r + lane).astype(BF16)
        h, m = split(tile)
        l = (tile - h.astype(F32) - m.astype(F32)).astype(BF16)
        return (
            lax.dot_general(pick, h, NT, preferred_element_type=F32)
            + lax.dot_general(pick, m, NT, preferred_element_type=F32)
            + lax.dot_general(pick, l, NT, preferred_element_type=F32)
        )[:2]

    el_ref[0] = edge(w_ref[:, :, :128].reshape(beams * rows, 128), 0)
    er_ref[0] = edge(w_ref[:, :, cols - 128 :].reshape(beams * rows, 128), 126)

    @pl.when(i == last)
    def _():
        n, m = acc_ref.shape
        kept = acc_ref[...] * one_hot(n, m, lambda r, c: r % 8 == c % 8)
        fold = one_hot(m, 128, lambda r, c: r // 8 == c)
        gather = one_hot(out_ref.shape[0], n, lambda r, c: c // 8 == r)
        half = jnp.dot(kept, fold, precision=lax.Precision.HIGHEST, preferred_element_type=F32)
        out_ref[...] = jnp.dot(gather, half, precision=lax.Precision.HIGHEST, preferred_element_type=F32)


def update_kernel(
    a_ref, b_ref, flag_ref, w_ref, wp_ref, wn_ref, wt_ref, wb_ref, halo_ref, x_ref, lx_ref, mix_ref,
    out_ref, tile_ref, mask_ref
):
    i, last = pl.program_id(0), pl.num_programs(0) - 1
    beams, rows, cols = w_ref.shape
    pool = x_ref.shape[0]
    width = cols + 128

    def make_tile(j):
        raw = halo_ref[j]
        h = raw.astype(BF16).astype(F32)
        m = (raw - h).astype(BF16).astype(F32)
        l = raw - h - m
        stack = jnp.concatenate([h, m, l, jnp.zeros_like(h)], axis=0)
        r = lax.broadcasted_iota(jnp.int32, (16, 128), 0)
        c = lax.broadcasted_iota(jnp.int32, (16, 128), 1)
        k = r % 4
        spot = jnp.where(k < 2, k + 126, k - 2)
        place = jnp.where((c == spot) & (r < 12), 1.0, 0.0).astype(BF16)
        tile = jnp.dot(stack.T.astype(BF16), place, preferred_element_type=F32)
        tile_ref[j % 3] = tile.reshape(beams, rows, 128)

    @pl.when(i == 0)
    def _():
        make_tile(0)
        make_tile(1)

    make_tile(i + 2)

    r = lax.broadcasted_iota(jnp.int32, (rows + 16, width), 0)
    c = lax.broadcasted_iota(jnp.int32, (rows + 16, width), 1)
    mask = jnp.ones((rows + 16, width), F32)
    mask = jnp.where((r < 8) & (i == 0), flag_ref[0], mask)
    mask = jnp.where((r >= rows + 8) & (i == last), flag_ref[1], mask)
    mask = mask * jnp.where(c >= cols + 64, flag_ref[2], 1.0)
    mask_ref[...] = mask * jnp.where((c >= cols) & (c < cols + 64), flag_ref[3], 1.0)

    for g in range(rows // 8):
        part = pl.ds(8 * g, 8)
        xg = x_ref[:, part, :].reshape(pool * 8, cols)
        lg = lx_ref[:, part, :].reshape(pool * 8, cols)
        rh, rl = split(jnp.concatenate([xg, lg], axis=0))
        full = jnp.concatenate([rh, rl, rh], axis=0)
        mixed = jnp.dot(mix_ref[...], full, preferred_element_type=F32)
        out_ref[:, part, :] = mixed.reshape(beams, 8, cols)

    before, here, after = lax.rem(i, 3), lax.rem(i + 1, 3), lax.rem(i + 2, 3)

    def beam(n, carry):
        cur = w_ref[n]
        a, b = a_ref[n], b_ref[n]

        def field():
            above = jnp.where(i == 0, wt_ref[n], wp_ref[n])
            below = jnp.where(i == last, wb_ref[n], wn_ref[n])
            main = jnp.concatenate([above, cur, below], axis=0)
            side = jnp.concatenate(
                [tile_ref[before, n, rows - 8 :], tile_ref[here, n], tile_ref[after, n, :8]], axis=0
            )
            return jnp.concatenate([main, side], axis=1)

        @pl.when(b == 0.0)
        def _():
            out_ref[n] += cur + a * laplacian(field())[8 : rows + 8, :cols]

        @pl.when(b != 0.0)
        def _():
            wide = field()
            q = a * wide + b * (laplacian(wide) * mask_ref[...])
            out_ref[n] += cur + laplacian(q)[8 : rows + 8, :cols]

        return carry

    lax.fori_loop(0, beams, beam, 0)


def shift_pair(first, final, axis):
    count = lax.axis_size(axis)
    up = [(i, i + 1) for i in range(count - 1)]
    down = [(i + 1, i) for i in range(count - 1)]
    return lax.ppermute(final, axis, up), lax.ppermute(first, axis, down)


def total(value):
    for axis in ("row", "col"):
        count = lax.axis_size(axis)
        if count & (count - 1):
            value = lax.psum(value, axis)
            continue
        hop = 1
        while hop < count:
            value = value + lax.ppermute(value, axis, [(i, i ^ hop) for i in range(count)])
            hop *= 2
    return value


def body(rows, weights, pool, desired, plan, beam_ref, step_size, smoothing, active):
    beams, height, cols = weights.shape
    count = pool.shape[0]
    blocks = height // rows
    eighths = rows // 8
    row_n, col_n = lax.axis_size("row"), lax.axis_size("col")
    row_i, col_i = lax.axis_index("row"), lax.axis_index("col")
    scale = 1.0 / math.sqrt(height * row_n * cols * col_n)
    high = lax.Precision.HIGHEST

    xt, xb = shift_pair(pool[:, :8], pool[:, -8:], "row")
    xl, xr = shift_pair(pool[:, :, 0], pool[:, :, -1], "col")
    lane = jnp.arange(128)[None, None, :]
    xe = jnp.where(lane == 0, xr[:, :, None], jnp.where(lane == 127, xl[:, :, None], 0.0))
    wt, wb = shift_pair(weights[:, :8], weights[:, -8:], "row")

    def block(n, r=rows, w=cols):
        return pl.BlockSpec((n, r, w), lambda i: (0, i, 0))

    def previous(n):
        return pl.BlockSpec((n, 8, cols), lambda i: (0, jnp.maximum(i * eighths - 1, 0), 0))

    def following(n):
        return pl.BlockSpec((n, 8, cols), lambda i: (0, jnp.minimum((i + 1) * eighths, blocks * eighths - 1), 0))

    def whole(*shape):
        return pl.BlockSpec(shape, lambda i: (0,) * len(shape))

    edges = pl.BlockSpec((1, 2, beams * rows), lambda i: (i, 0, 0))
    planes = -(-(beams + count) // 8) * 8
    sums, lx, first, final = pl.pallas_call(
        moments_kernel,
        grid=(blocks,),
        in_specs=[block(beams), block(count), previous(count), following(count), whole(count, 8, cols),
                  whole(count, 8, cols), block(count, rows, 128)],
        out_specs=[whole(planes, 128), block(count), edges, edges],
        out_shape=[
            jax.ShapeDtypeStruct((planes, 128), F32),
            jax.ShapeDtypeStruct(pool.shape, F32),
            jax.ShapeDtypeStruct((blocks, 2, beams * rows), F32),
            jax.ShapeDtypeStruct((blocks, 2, beams * rows), F32),
        ],
        scratch_shapes=[pltpu.VMEM(((beams + count) * 8, 2 * count * 8), F32)],
        compiler_params=pltpu.CompilerParams(vmem_limit_bytes=LIMIT),
        cost_estimate=pl.CostEstimate(flops=10**10, bytes_accessed=10**8, transcendentals=0),
        name="moments",
    )(weights, pool, pool, pool, xt, xb, xe)

    left, right = shift_pair(first, final, "col")
    halo = jnp.concatenate([left, right], axis=1)
    top, bottom = shift_pair(halo[:1], halo[-1:], "row")
    halo = jnp.concatenate([top, halo, bottom], axis=0)

    sums = total(sums)
    gram, lapped, cross = sums[:beams, :count], sums[:beams, count : 2 * count], sums[beams : beams + count, :count]
    refs = desired.shape[1]
    pick = (beam_ref[:, None] == jnp.arange(refs, dtype=jnp.int32)[None, :]).astype(F32)
    targets = jnp.dot(pick, desired.T, precision=high)
    rate = (step_size * scale)[:, None]
    chosen = [(plan[t][None, :] == jnp.arange(count, dtype=jnp.int32)[:, None]).astype(F32) for t in range(2)]
    live = [(active > t).astype(F32)[:, None] for t in range(2)]
    s0, s1 = (live[t] * smoothing[:, None] for t in range(2))

    error0 = jnp.dot(targets - scale * gram, chosen[0], precision=high)
    c0 = live[0] * rate * jnp.dot(error0, chosen[0].T, precision=high)
    later = gram + s0 * lapped + jnp.dot(c0, cross, precision=high)
    error1 = jnp.dot(targets - scale * later, chosen[1], precision=high)
    c1 = live[1] * rate * jnp.dot(error1, chosen[1].T, precision=high)

    mix = jnp.concatenate([c0 + c1, s1 * c0], axis=1)
    mix = (mix[:, None, :, None] * jnp.eye(8, dtype=F32)[None, :, None, :]).reshape(beams * 8, 2 * count * 8)
    mix_hi = lax.reduce_precision(mix, 8, 7)
    mix_lo = (mix - mix_hi).astype(BF16)
    mix_hi = mix_hi.astype(BF16)
    mix = jnp.concatenate([mix_hi, mix_hi, mix_lo], axis=1)
    flags = jnp.stack([row_i > 0, row_i < row_n - 1, col_i > 0, col_i < col_n - 1]).astype(F32)

    smem = pl.BlockSpec(memory_space=pltpu.SMEM)
    out = pl.pallas_call(
        update_kernel,
        grid=(blocks,),
        in_specs=[smem, smem, smem, block(beams), previous(beams), following(beams), whole(beams, 8, cols),
                  whole(beams, 8, cols), whole(blocks + 2, 4, beams * rows), block(count), block(count),
                  whole(beams * 8, 6 * count * 8)],
        out_specs=block(beams),
        out_shape=jax.ShapeDtypeStruct(weights.shape, F32),
        scratch_shapes=[pltpu.VMEM((3, beams, rows, 128), F32), pltpu.VMEM((rows + 16, cols + 128), F32)],
        compiler_params=pltpu.CompilerParams(vmem_limit_bytes=LIMIT),
        cost_estimate=pl.CostEstimate(flops=10**10, bytes_accessed=10**8, transcendentals=0),
        name="update",
    )((s0 + s1)[:, 0], (s0 * s1)[:, 0], flags, weights, weights, weights, wt, wb, halo, pool, lx, mix)
    return out, jnp.stack([error0, error1])


def solution(mesh):
    in_specs = (P(None, "row", "col"), P(None, "row", "col"), P(), P(), P(), P(), P(), P())
    out_specs = (P(None, "row", "col"), P())
    return jax.shard_map(functools.partial(body, 32), mesh=mesh, in_specs=in_specs, out_specs=out_specs, check_vma=False)
```

time: 725 us -> 275 us (0.38)
  matrix products: 353 us -> 1.11 us
  local copies, waits for them, and re-layouts: 217 us -> 20.3 us
  Pallas kernels: 0 us -> 191 us
  blocking collectives: 78.2 us -> 0 us
  other arithmetic: 42.9 us -> 11.3 us
  starting transfers between devices: 26.3 us -> 39.4 us
    dot_general x7 -> x6, matrix products: 353 us -> 1.11 us  [the longest x1 0.24 us: body(): later = gram + s0 * lapped + jnp.dot(c0, cross, precision=high)]
    pallas_call x0 -> x2, Pallas kernels: none -> 191 us  [the longest x1 150 us: body(): pl.pallas_call(update_kernel, grid=(blocks,), in_specs=[smem, smem, smem,...]
    unnamed x22, local copies, waits for them, and re-layouts: 117 us -> 7.57 us
    psum x2 -> x0, blocking collectives: 78.2 us -> none  [beam_sum(): return lax.psum(local, ('row', 'col')) * scale]
    slice x7 -> x3, local copies, waits for them, and re-layouts: 46.8 us -> 9.71 us  [the longest x1 5.47 us: body(): xl, xr = shift_pair(pool[:, :, 0], pool[:, :, -1], 'col')]
    ppermute x4 -> x0, local copies, waits for them, and re-layouts: 26.7 us -> none  [the longest x2 13.5 us: padded_2(): after = lax.ppermute(leading, axis, down)]
    gather x2 -> x0, local copies, waits for them, and re-layouts: 25.4 us -> none  [body(): snaps = jnp.take(pool, plan[step], axis=0)]
    select_n x2 -> x1, other arithmetic: 23.9 us -> 4.13 us  [body(): jnp.where(lane == 0, xr[:, :, None], jnp.where(lane == 127, xl[:, :, None...]
  transfers between devices with their start and end apart: 8 -> 15, of which waited for: 0 -> 5; matrix products, arithmetic and copies ran while one was open for 32% -> 11% of each run, Pallas kernels for 0% -> 15%
where the time goes in v1:
time: 275 us; the launch traced here: 271 us
  Pallas kernels  191 us (69%)
  starting transfers between devices  39.4 us (14%)
  local copies, waits for them, and re-layouts  20.3 us (7%)
  other arithmetic  11.3 us (4%)
  waiting for transfers between devices  7.02 us (3%)
    pallas_call x1, Pallas kernels, body(): pl.pallas_call(update_kernel, grid=(blocks,), in_specs=[smem, smem, smem,...  150 us
    pallas_call x1, Pallas kernels, body(): pl.pallas_call(moments_kernel, grid=(blocks,), in_specs=[block(beams), bl...  41 us
    ppermute x10, starting transfers between devices, shift_pair(): return (lax.ppermute(final, axis, up), lax.ppermute(first, axis, down))  31.2 us
    ppermute x5, starting transfers between devices, total(): lax.ppermute(value, axis, [(i, i ^ hop) for i in range(count)])  8.23 us
    unnamed x22, local copies, waits for them, and re-layouts  7.57 us
  transfers between devices with their start and end apart: 15, of which 5 were waited for; matrix products, arithmetic and copies ran while one was open for 11% of the time, Pallas kernels for 15%

profile of v1, /device:TPU:1, one launch (start us, length us, event | category | flops | bytes accessed | tf_op | source)
XLA Modules:
  0.0 271.4 jit_solution(7363555265402148546)
XLA Ops:
  0.6 0.0 copy-start
  0.6 1.8 fusion.29
  2.4 2.0 collective-permute-start.3
  4.4 4.5 %collective-permute-start.2 = (f32[12,8,512]{2,1,0:T(8,128)}, f32[12,8,512]{2,1,0:T(8,128)S(1)}, u32[]{:S(2)}, u32[]{:S(2)}) collective-permute-start(f32[12,8,512]{2,1,0:T(8,128)} %get-tuple-element.18), channel_id=1, source_target_pairs={{0,8},{8,16},{16,24},{1,9},{9,17},{17,25},{2,10},{10,18},{18,26},{... | collective-permute-start | bytes 589832 | tf_op jit(solution)/shard_map/ppermute | solution.py:170
  8.9 2.4 fusion.27
  11.3 1.9 collective-permute-start.1
  13.3 5.5 %fusion.28 = (f32[12,512,1]{2,1,0:T(8,128)S(1)}, f32[12,512,1]{2,1,0:T(8,128)}) fusion(f32[12,512,512]{2,1,0:T(8,128)} %x_ref.3), kind=kLoop, calls=%fused_computation.53 | loop fusion | bytes 98304 | tf_op jit(solution)/shard_map/slice | solution.py:197
  18.7 3.3 %copy.30 = f32[12,512,1]{1,0,2:T(8,128)} copy(f32[12,512,1]{2,1,0:T(8,128)} %get-tuple-element.16) | data formatting | bytes 49152
  22.0 3.7 %collective-permute-start.5 = (f32[12,512]{1,0:T(8,128)}, f32[12,512]{1,0:T(8,128)}, u32[]{:S(2)}, u32[]{:S(2)}) collective-permute-start(f32[12,512]{1,0:T(8,128)} %bitcast.23), channel_id=1, source_target_pairs={{0,1},{1,2},{2,3},{3,4},{4,5},{5,6},{6,7},{8,9},{9,10},{10,11},{11... | collective-permute-start | bytes 73736 | tf_op jit(solution)/shard_map/ppermute | solution.py:170
  25.7 2.1 copy.29
  27.8 1.3 collective-permute-start.4
  29.1 0.0 collective-permute-done.5
  29.1 3.9 %collective-permute-start = (f32[40,8,512]{2,1,0:T(8,128)}, f32[40,8,512]{2,1,0:T(8,128)S(1)}, u32[]{:S(2)}, u32[]{:S(2)}) collective-permute-start(f32[40,8,512]{2,1,0:T(8,128)} %get-tuple-element.14), channel_id=1, source_target_pairs={{0,8},{8,16},{16,24},{1,9},{9,17},{17,25},{2,10},{10,18},{18,26},{... | collective-permute-start | bytes 1966088 | tf_op jit(solution)/shard_map/ppermute | solution.py:170
  33.0 0.0 collective-permute-done.4
  33.0 4.1 %select_select_fusion.xe_ref = f32[12,512,128]{2,1,0:T(8,128)} fusion(f32[12,512]{1,0:T(8,128)} %collective-permute-done.5, f32[12,512]{1,0:T(8,128)S(1)} %collective-permute-done.4, pred[128]{0:T(512)(128)(4,1)S(1)} %get-tuple-element.32, pred[128]{0:T(512)(128)(4,1)S(1)} %get-tuple-element.33), kind=kLoop, calls=%fused_computation | loop fusion | flops 1572864 | bytes 3195136 | tf_op jit(solution)/shard_map/jit(_where)/select_n | solution.py:199
  37.2 0.0 copy-start.5
  37.2 0.0 collective-permute-done.3.xb_ref
  37.2 0.0 copy-start.3
  37.2 0.0 collective-permute-done.2.xt_ref
  37.2 0.7 copy-done.3
  37.9 0.7 copy-done.4
  38.6 41.0 %moments.1 = (f32[56,128]{1,0:T(8,128)}, f32[12,512,512]{2,1,0:T(8,128)}, f32[16,2,1280]{2,1,0:T(2,128)}, f32[16,2,1280]{2,1,0:T(2,128)}) custom-call(f32[40,512,512]{2,1,0:T(8,128)} %wn_ref.1, f32[12,512,512]{2,1,0:T(8,128)} %x_ref.3, f32[12,512,512]{2,1,0:T(8,128)} %x_ref.3, f32[12,512,512]{2,1,0:T(8,128)} %x_ref.3, f32[12,8,512]{2,1,0:T(8,128)} %copy-done.4, ...), custom_call_target="tpu_custom_call" | custom-call | flops 10000000000 | bytes 100000000 | tf_op jit(solution)/shard_map/moments/pallas_call | solution.py:216
  79.6 0.1 collective-permute-start.10
  79.7 0.0 copy-done
  79.7 0.2 fusion.10
  79.9 1.2 collective-permute-done.10
  81.0 0.8 add.29
  81.8 2.5 collective-permute-start.11
  84.3 0.0 copy-done.8
  84.3 0.5 compare_select_fusion
  84.8 0.8 collective-permute-done.11
  85.6 1.6 collective-permute-start.12
  87.2 1.3 collective-permute-done.12
  88.4 1.6 collective-permute-start.13
  90.0 1.3 collective-permute-done.13
  91.3 2.5 collective-permute-start.14
  93.8 0.6 add_convert_fusion.flag_ref
  94.4 0.5 add.28.a_ref
  94.9 3.1 %collective-permute-start.6 = (f32[16,2,1280]{2,1,0:T(2,128)}, f32[16,2,1280]{2,1,0:T(2,128)S(1)}, u32[]{:S(2)}, u32[]{:S(2)}) collective-permute-start(f32[16,2,1280]{2,1,0:T(2,128)} %get-tuple-element.6), channel_id=1, source_target_pairs={{0,1},{1,2},{2,3},{3,4},{4,5},{5,6},{6,7},{8,9},{9,10},{10,11},{11... | collective-permute-start | bytes 491528 | tf_op jit(solution)/shard_map/ppermute | solution.py:170
  98.0 1.3 collective-permute-start.7
  99.3 0.0 collective-permute-done.14
  99.3 0.2 fusion.7
  99.5 0.1 broadcast_multiply_fusion.1
  99.6 0.2 fusion.17
  99.9 0.2 fusion.5
  100.1 0.1 fusion
  100.2 2.2 broadcast_multiply_fusion
  102.5 2.7 mul.101
  105.2 0.1 copy.25
  105.4 0.1 copy.24
  105.5 0.1 fusion.30
  105.6 0.9 pad_maximum_fusion.mix_ref
  106.5 0.0 collective-permute-done.6
  106.5 0.0 collective-permute-done.7
  106.5 7.6 %collective-permute-start.8 = (f32[1,4,1280]{2,1,0:T(4,128)S(1)}, f32[1,4,1280]{2,1,0:T(4,128)S(1)}, u32[]{:S(2)}, u32[]{:S(2)}) collective-permute-start(f32[1,4,1280]{2,1,0:T(4,128)S(1)} %get-tuple-element.21), channel_id=1, source_target_pairs={{0,8},{8,16},{16,24},{1,9},{9,17},{17,25},{2,10},{10,18},{18,26},{... | collective-permute-start | bytes 61448 | tf_op jit(solution)/shard_map/ppermute | solution.py:170
  114.1 1.9 collective-permute-start.9
  116.1 0.6 pad_maximum_fusion.4
  116.7 0.0 collective-permute-done.8
  116.7 2.6 collective-permute-done.9
  119.2 0.9 pad_maximum_fusion.1.halo_ref
  120.1 0.0 collective-permute-done.1.wb_ref
  120.2 0.0 collective-permute-done.wt_ref
  120.2 0.9 copy-done.2
  121.0 150.4 %update.1 = f32[40,512,512]{2,1,0:T(8,128)} custom-call(f32[40]{0:T(128)} %add.28.a_ref, f32[40]{0:T(128)} %get-tuple-element.27.b_ref, f32[4]{0:T(128)} %add_convert_fusion.flag_ref, f32[40,512,512]{2,1,0:T(8,128)} %wn_ref.1, f32[40,512,512]{2,1,0:T(8,128)} %wn_ref.1, f32[40,512,512]{2,1,0:T(8,128)} %wn_ref.1, f32[40,8,512]{2,1,0:T(8,128)} %copy-done.2, ...), custom_call_target="tpu_custom_call" | custom-call | flops 10000000000 | bytes 100000000 | tf_op jit(solution)/shard_map/update/pallas_call | solution.py:264
  (22 shorter events, 0.1 us)
Async XLA Ops:
  0.6 79.0 %copy-start = (f32[12,8]{0,1:T(8,128)S(1)}, f32[12,8]{0,1:T(8,128)}, u32[]{:S(2)}) copy-start(f32[12,8]{0,1:T(8,128)} %param.10) | copy-start | bytes 1156
  2.4 34.8 %collective-permute-start.3 = (f32[12,8,512]{2,1,0:T(8,128)}, f32[12,8,512]{2,1,0:T(8,128)S(1)}, u32[]{:S(2)}, u32[]{:S(2)}) collective-permute-start(f32[12,8,512]{2,1,0:T(8,128)} %get-tuple-element.17), channel_id=1, source_target_pairs={{8,0},{16,8},{24,16},{9,1},{17,9},{25,17},{10,2},{18,10},{26,18},{... | collective-permute-start | bytes 589832 | tf_op jit(solution)/shard_map/ppermute | solution.py:170
  4.4 32.8 %collective-permute-start.2 = (f32[12,8,512]{2,1,0:T(8,128)}, f32[12,8,512]{2,1,0:T(8,128)S(1)}, u32[]{:S(2)}, u32[]{:S(2)}) collective-permute-start(f32[12,8,512]{2,1,0:T(8,128)} %get-tuple-element.18), channel_id=1, source_target_pairs={{0,8},{8,16},{16,24},{1,9},{9,17},{17,25},{2,10},{10,18},{18,26},{... | collective-permute-start | bytes 589832 | tf_op jit(solution)/shard_map/ppermute | solution.py:170
  11.3 108.8 %collective-permute-start.1 = (f32[40,8,512]{2,1,0:T(8,128)}, f32[40,8,512]{2,1,0:T(8,128)}, u32[]{:S(2)}, u32[]{:S(2)}) collective-permute-start(f32[40,8,512]{2,1,0:T(8,128)} %get-tuple-element.13), channel_id=1, source_target_pairs={{8,0},{16,8},{24,16},{9,1},{17,9},{25,17},{10,2},{18,10},{26,18},{... | collective-permute-start | bytes 1966088 | tf_op jit(solution)/shard_map/ppermute | solution.py:170
  22.0 7.1 %collective-permute-start.5 = (f32[12,512]{1,0:T(8,128)}, f32[12,512]{1,0:T(8,128)}, u32[]{:S(2)}, u32[]{:S(2)}) collective-permute-start(f32[12,512]{1,0:T(8,128)} %bitcast.23), channel_id=1, source_target_pairs={{0,1},{1,2},{2,3},{3,4},{4,5},{5,6},{6,7},{8,9},{9,10},{10,11},{11... | collective-permute-start | bytes 73736 | tf_op jit(solution)/shard_map/ppermute | solution.py:170
  27.8 5.2 %collective-permute-start.4 = (f32[12,512]{1,0:T(8,128)}, f32[12,512]{1,0:T(8,128)S(1)}, u32[]{:S(2)}, u32[]{:S(2)}) collective-permute-start(f32[12,512]{1,0:T(8,128)} %bitcast.22), channel_id=1, source_target_pairs={{1,0},{2,1},{3,2},{4,3},{5,4},{6,5},{7,6},{9,8},{10,9},{11,10},{12... | collective-permute-start | bytes 73736 | tf_op jit(solution)/shard_map/ppermute | solution.py:170
  29.1 91.0 %collective-permute-start = (f32[40,8,512]{2,1,0:T(8,128)}, f32[40,8,512]{2,1,0:T(8,128)S(1)}, u32[]{:S(2)}, u32[]{:S(2)}) collective-permute-start(f32[40,8,512]{2,1,0:T(8,128)} %get-tuple-element.14), channel_id=1, source_target_pairs={{0,8},{8,16},{16,24},{1,9},{9,17},{17,25},{2,10},{10,18},{18,26},{... | collective-permute-start | bytes 1966088 | tf_op jit(solution)/shard_map/ppermute | solution.py:170
  37.2 42.5 %copy-start.9 = (s32[40]{0:T(128)S(1)}, s32[40]{0:T(128)}, u32[]{:S(2)}) copy-start(s32[40]{0:T(128)} %param.12) | copy-start | bytes 484
  37.2 47.2 %copy-start.6 = (s32[40]{0:T(128)S(1)}, s32[40]{0:T(128)}, u32[]{:S(2)}) copy-start(s32[40]{0:T(128)} %param.15) | copy-start | bytes 484
  37.2 47.2 %copy-start.7 = (f32[40]{0:T(128)S(1)}, f32[40]{0:T(128)}, u32[]{:S(2)}) copy-start(f32[40]{0:T(128)} %param.13) | copy-start | bytes 484
  37.2 47.2 %copy-start.8 = (f32[40]{0:T(128)S(1)}, f32[40]{0:T(128)}, u32[]{:S(2)}) copy-start(f32[40]{0:T(128)} %param.14) | copy-start | bytes 484
  37.2 50.0 %copy-start.5 = (s32[2,16]{1,0:T(2,128)S(1)}, s32[2,16]{1,0:T(2,128)}, u32[]{:S(2)}) copy-start(s32[2,16]{1,0:T(2,128)} %param.11) | copy-start | bytes 388
  37.2 0.7 copy-start.3
  37.9 0.7 copy-start.4
  79.6 1.5 collective-permute-start.10
  81.8 3.8 %collective-permute-start.11 = (f32[56,128]{1,0:T(8,128)S(1)}, f32[56,128]{1,0:T(8,128)S(1)}, u32[]{:S(2)}, u32[]{:S(2)}) collective-permute-start(f32[56,128]{1,0:T(8,128)S(1)} %add.29), channel_id=1, source_target_pairs={{0,16},{8,24},{16,0},{24,8},{1,17},{9,25},{17,1},{25,9},{2,18},{10... | collective-permute-start | bytes 86024 | tf_op jit(solution)/shard_map/ppermute | solution.py:181
  85.6 2.8 %collective-permute-start.12 = (f32[56,128]{1,0:T(8,128)S(1)}, f32[56,128]{1,0:T(8,128)S(1)}, u32[]{:S(2)}, u32[]{:S(2)}) collective-permute-start(f32[56,128]{1,0:T(8,128)S(1)} %add.30), channel_id=1, source_target_pairs={{0,1},{1,0},{2,3},{3,2},{4,5},{5,4},{6,7},{7,6},{8,9},{9,8},{10,11... | collective-permute-start | bytes 86024 | tf_op jit(solution)/shard_map/ppermute | solution.py:181
  88.4 2.8 %collective-permute-start.13 = (f32[56,128]{1,0:T(8,128)S(1)}, f32[56,128]{1,0:T(8,128)S(1)}, u32[]{:S(2)}, u32[]{:S(2)}) collective-permute-start(f32[56,128]{1,0:T(8,128)S(1)} %add.31), channel_id=1, source_target_pairs={{0,2},{1,3},{2,0},{3,1},{4,6},{5,7},{6,4},{7,5},{8,10},{9,11},{10,... | collective-permute-start | bytes 86024 | tf_op jit(solution)/shard_map/ppermute | solution.py:181
  91.3 8.0 %collective-permute-start.14 = (f32[56,128]{1,0:T(8,128)S(1)}, f32[56,128]{1,0:T(8,128)S(1)}, u32[]{:S(2)}, u32[]{:S(2)}) collective-permute-start(f32[56,128]{1,0:T(8,128)S(1)} %add.32), channel_id=1, source_target_pairs={{0,4},{1,5},{2,6},{3,7},{4,0},{5,1},{6,2},{7,3},{8,12},{9,13},{10,... | collective-permute-start | bytes 86024 | tf_op jit(solution)/shard_map/ppermute | solution.py:181
  94.9 11.6 %collective-permute-start.6 = (f32[16,2,1280]{2,1,0:T(2,128)}, f32[16,2,1280]{2,1,0:T(2,128)S(1)}, u32[]{:S(2)}, u32[]{:S(2)}) collective-permute-start(f32[16,2,1280]{2,1,0:T(2,128)} %get-tuple-element.6), channel_id=1, source_target_pairs={{0,1},{1,2},{2,3},{3,4},{4,5},{5,6},{6,7},{8,9},{9,10},{10,11},{11... | collective-permute-start | bytes 491528 | tf_op jit(solution)/shard_map/ppermute | solution.py:170
  98.0 8.5 %collective-permute-start.7 = (f32[16,2,1280]{2,1,0:T(2,128)}, f32[16,2,1280]{2,1,0:T(2,128)S(1)}, u32[]{:S(2)}, u32[]{:S(2)}) collective-permute-start(f32[16,2,1280]{2,1,0:T(2,128)} %get-tuple-element.7), channel_id=1, source_target_pairs={{1,0},{2,1},{3,2},{4,3},{5,4},{6,5},{7,6},{9,8},{10,9},{11,10},{12... | collective-permute-start | bytes 491528 | tf_op jit(solution)/shard_map/ppermute | solution.py:170
  106.5 10.2 %collective-permute-start.8 = (f32[1,4,1280]{2,1,0:T(4,128)S(1)}, f32[1,4,1280]{2,1,0:T(4,128)S(1)}, u32[]{:S(2)}, u32[]{:S(2)}) collective-permute-start(f32[1,4,1280]{2,1,0:T(4,128)S(1)} %get-tuple-element.21), channel_id=1, source_target_pairs={{0,8},{8,16},{16,24},{1,9},{9,17},{17,25},{2,10},{10,18},{18,26},{... | collective-permute-start | bytes 61448 | tf_op jit(solution)/shard_map/ppermute | solution.py:170
  114.1 5.1 %collective-permute-start.9 = (f32[1,4,1280]{2,1,0:T(4,128)S(1)}, f32[1,4,1280]{2,1,0:T(4,128)S(1)}, u32[]{:S(2)}, u32[]{:S(2)}) collective-permute-start(f32[1,4,1280]{2,1,0:T(4,128)S(1)} %get-tuple-element.22), channel_id=1, source_target_pairs={{8,0},{16,8},{24,16},{9,1},{17,9},{25,17},{10,2},{18,10},{26,18},{... | collective-permute-start | bytes 61448 | tf_op jit(solution)/shard_map/ppermute | solution.py:170
  120.2 0.9 copy-start.2
  121.0 150.4 %copy-start.1 = (f32[12,8]{0,1:T(8,128)S(1)}, f32[12,8]{0,1:T(8,128)}, u32[]{:S(2)}) copy-start(f32[12,8]{0,1:T(8,128)} %param.10) | copy-start | bytes 1156

commit v2 on v1

--- a/solution.py
+++ b/solution.py
@@ -23,10 +23,6 @@
 def neighbours(x, axis):
     size = x.shape[axis]
     return pltpu.roll(x, 1, axis) + pltpu.roll(x, size - 1, axis)
-
-
-def laplacian(x):
-    return neighbours(x, 0) + neighbours(x, 1) - 4.0 * x
 
 
 def one_hot(rows, cols, hit):
@@ -87,13 +83,13 @@
 
 
 def update_kernel(
-    a_ref, b_ref, flag_ref, w_ref, wp_ref, wn_ref, wt_ref, wb_ref, halo_ref, x_ref, lx_ref, mix_ref,
-    out_ref, tile_ref, mask_ref
+    a_ref, b_ref, flag_ref, w_ref, wp_ref, wn_ref, wt_ref, wb_ref, halo_ref, x_ref, lx_ref, coef_ref,
+    out_ref, tile_ref, mask_ref, mix_ref, s_ref, q_ref
 ):
     i, last = pl.program_id(0), pl.num_programs(0) - 1
     beams, rows, cols = w_ref.shape
     pool = x_ref.shape[0]
-    width = cols + 128
+    tiles = cols // 128
 
     def make_tile(j):
         raw = halo_ref[j]
@@ -113,16 +109,22 @@
     def _():
         make_tile(0)
         make_tile(1)
+        n, m = beams * 8, 2 * pool * 8
+        down = one_hot(n, beams, lambda r, c: r // 8 == c)
+        along = one_hot(2 * pool, m, lambda r, c: r == c // 8)
+        full = jnp.dot(down, coef_ref[...], precision=lax.Precision.HIGHEST, preferred_element_type=F32)
+        full = jnp.dot(full, along, precision=lax.Precision.HIGHEST, preferred_element_type=F32)
+        high, low = split(full * one_hot(n, m, lambda r, c: r % 8 == c % 8))
+        mix_ref[...] = jnp.concatenate([high, high, low], axis=1)
 
     make_tile(i + 2)
 
-    r = lax.broadcasted_iota(jnp.int32, (rows + 16, width), 0)
-    c = lax.broadcasted_iota(jnp.int32, (rows + 16, width), 1)
-    mask = jnp.ones((rows + 16, width), F32)
-    mask = jnp.where((r < 8) & (i == 0), flag_ref[0], mask)
-    mask = jnp.where((r >= rows + 8) & (i == last), flag_ref[1], mask)
-    mask = mask * jnp.where(c >= cols + 64, flag_ref[2], 1.0)
-    mask_ref[...] = mask * jnp.where((c >= cols) & (c < cols + 64), flag_ref[3], 1.0)
+    r = lax.broadcasted_iota(jnp.int32, (rows + 8, 128), 0)
+    c = lax.broadcasted_iota(jnp.int32, (rows + 8, 128), 1)
+    mask = jnp.where((r == 0) & (i == 0), flag_ref[0], 1.0)
+    mask = jnp.where((r == rows + 1) & (i == last), flag_ref[1], mask)
+    mask_ref[0] = mask
+    mask_ref[1] = mask * jnp.where(c >= 64, flag_ref[2], flag_ref[3])
 
     for g in range(rows // 8):
         part = pl.ds(8 * g, 8)
@@ -135,32 +137,151 @@
 
     before, here, after = lax.rem(i, 3), lax.rem(i + 1, 3), lax.rem(i + 2, 3)
 
+    def across(parts, count):
+        lane = lax.broadcasted_iota(jnp.int32, parts[0].shape, 1)
+        one = [pltpu.roll(v, 1, 1) for v in parts]
+        two = [pltpu.roll(v, 127, 1) for v in parts]
+        n = len(parts)
+        return [
+            jnp.where(lane == 0, one[k - 1], one[k]) + jnp.where(lane == 127, two[(k + 1) % n], two[k])
+            for k in range(count)
+        ]
+
+    def lap_rows(ref, start, size, count):
+        mid = [ref[k, pl.ds(start, size)] for k in range(tiles + 1)]
+        side = across(mid, count)
+        laps = [
+            ref[k, pl.ds(start - 1, size)] + ref[k, pl.ds(start + 1, size)] + side[k] - 4.0 * mid[k]
+            for k in range(count)
+        ]
+        return mid, laps
+
     def beam(n, carry):
-        cur = w_ref[n]
         a, b = a_ref[n], b_ref[n]
-
-        def field():
-            above = jnp.where(i == 0, wt_ref[n], wp_ref[n])
-            below = jnp.where(i == last, wb_ref[n], wn_ref[n])
-            main = jnp.concatenate([above, cur, below], axis=0)
-            side = jnp.concatenate(
-                [tile_ref[before, n, rows - 8 :], tile_ref[here, n], tile_ref[after, n, :8]], axis=0
-            )
-            return jnp.concatenate([main, side], axis=1)
+        for k in range(tiles):
+            lanes = pl.ds(128 * k, 128)
+            s_ref[k, pl.ds(0, 8)] = jnp.where(i == 0, wt_ref[n, :, lanes], wp_ref[n, :, lanes])
+            s_ref[k, pl.ds(8, rows)] = w_ref[n, :, lanes]
+            s_ref[k, pl.ds(rows + 8, 8)] = jnp.where(i == last, wb_ref[n, :, lanes], wn_ref[n, :, lanes])
+        s_ref[tiles, pl.ds(0, 8)] = tile_ref[before, n, pl.ds(rows - 8, 8)]
+        s_ref[tiles, pl.ds(8, rows)] = tile_ref[here, n]
+        s_ref[tiles, pl.ds(rows + 8, 8)] = tile_ref[after, n, pl.ds(0, 8)]
 
         @pl.when(b == 0.0)
         def _():
-            out_ref[n] += cur + a * laplacian(field())[8 : rows + 8, :cols]
+            for t in range(0, rows, 16):
+                mid, laps = lap_rows(s_ref, 8 + t, 16, tiles)
+                for k in range(tiles):
+                    spot = (n, pl.ds(t, 16), pl.ds(128 * k, 128))
+                    out_ref[spot] = out_ref[spot] + mid[k] + a * laps[k]
 
         @pl.when(b != 0.0)
         def _():
-            wide = field()
-            q = a * wide + b * (laplacian(wide) * mask_ref[...])
-            out_ref[n] += cur + laplacian(q)[8 : rows + 8, :cols]
+            for t in range(0, rows + 8, 24):
+                mid, laps = lap_rows(s_ref, 7 + t, 24, tiles + 1)
+                for k in range(tiles + 1):
+                    kept = laps[k] * mask_ref[k // tiles, pl.ds(t, 24)]
+                    q_ref[k, pl.ds(t, 24)] = a * mid[k] + b * kept
+            for t in range(0, rows, 16):
+                _, laps = lap_rows(q_ref, 1 + t, 16, tiles)
+                for k in range(tiles):
+                    spot = (n, pl.ds(t, 16), pl.ds(128 * k, 128))
+                    out_ref[spot] = out_ref[spot] + w_ref[spot] + laps[k]
 
         return carry
 
     lax.fori_loop(0, beams, beam, 0)
+
+
+def share_kernel(
+    row_n, col_n, sums_ref, first_ref, final_ref, out_ref, halo_ref,
+    held, got, left_in, right_in, corner_up, corner_down, corner_top, corner_bottom,
+    send, recv, edge_send, edge_recv
+):
+    row, col = lax.axis_index("row"), lax.axis_index("col")
+    blocks = first_ref.shape[0]
+
+    def partner(me, hop):
+        return me + hop - 2 * hop * lax.rem(lax.div(me, hop), 2)
+
+    hops = []
+    for hop in [1 << k for k in range(row_n.bit_length() - 1)]:
+        hops.append((partner(row, hop), col))
+    for hop in [1 << k for k in range(col_n.bit_length() - 1)]:
+        hops.append((row, partner(col, hop)))
+    right = (row, lax.rem(col + 1, col_n))
+    left = (row, lax.rem(col + col_n - 1, col_n))
+    below = (lax.rem(row + 1, row_n), col)
+    above = (lax.rem(row + row_n - 1, row_n), col)
+
+    barrier = pltpu.get_barrier_semaphore()
+    others = hops + [right, left, below, above]
+    for other in others:
+        pl.semaphore_signal(barrier, inc=1, device_id=other, device_id_type=pl.DeviceIdType.MESH)
+    pl.semaphore_wait(barrier, len(others))
+
+    def copy(src, dst, s, r, device):
+        return pltpu.make_async_remote_copy(
+            src_ref=src, dst_ref=dst, send_sem=s, recv_sem=r, device_id=device,
+            device_id_type=pl.DeviceIdType.MESH,
+        )
+
+    to_right = copy(final_ref, left_in, edge_send.at[0], edge_recv.at[0], right)
+    to_left = copy(first_ref, right_in, edge_send.at[1], edge_recv.at[1], left)
+    held[0] = sums_ref[...]
+    for k, other in enumerate(hops):
+        move = copy(held.at[k], got.at[k], send.at[k], recv.at[k], other)
+        move.start()
+        if k == 0:
+            to_right.start()
+            to_left.start()
+        move.wait()
+        held[k + 1] = held[k] + got[k]
+    out_ref[...] = held[len(hops)]
+
+    to_right.wait()
+    to_left.wait()
+    halo_ref[pl.ds(1, blocks), pl.ds(0, 2)] = jnp.where(col > 0, left_in[...], 0.0)
+    halo_ref[pl.ds(1, blocks), pl.ds(2, 2)] = jnp.where(col < col_n - 1, right_in[...], 0.0)
+    corner_up[...] = halo_ref[1]
+    corner_down[...] = halo_ref[blocks]
+    down = copy(corner_down, corner_top, edge_send.at[2], edge_recv.at[2], below)
+    up = copy(corner_up, corner_bottom, edge_send.at[3], edge_recv.at[3], above)
+    down.start()
+    up.start()
+    down.wait()
+    up.wait()
+    halo_ref[0] = jnp.where(row > 0, corner_top[...], 0.0)
+    halo_ref[blocks + 1] = jnp.where(row < row_n - 1, corner_bottom[...], 0.0)
+
+
+def share(sums, first, final):
+    row_n, col_n = lax.axis_size("row"), lax.axis_size("col")
+    blocks, _, length = first.shape
+    hops = row_n.bit_length() + col_n.bit_length() - 2
+    vmem = pl.BlockSpec(memory_space=pltpu.VMEM)
+    return pl.pallas_call(
+        functools.partial(share_kernel, row_n, col_n),
+        in_specs=[vmem] * 3,
+        out_specs=[vmem] * 2,
+        out_shape=[jax.ShapeDtypeStruct(sums.shape, F32), jax.ShapeDtypeStruct((blocks + 2, 4, length), F32)],
+        scratch_shapes=[
+            pltpu.VMEM((hops + 1, *sums.shape), F32),
+            pltpu.VMEM((hops, *sums.shape), F32),
+            pltpu.VMEM(first.shape, F32),
+            pltpu.VMEM(first.shape, F32),
+            *[pltpu.VMEM((4, length), F32) for _ in range(4)],
+            pltpu.SemaphoreType.DMA((hops,)),
+            pltpu.SemaphoreType.DMA((hops,)),
+            pltpu.SemaphoreType.DMA((4,)),
+            pltpu.SemaphoreType.DMA((4,)),
+        ],
+        compiler_params=pltpu.CompilerParams(
+            collective_id=0, has_side_effects=True, vmem_limit_bytes=LIMIT
+        ),
+        cost_estimate=pl.CostEstimate(flops=10**6, bytes_accessed=10**7, transcendentals=0),
+        name="share",
+    )(sums, first, final)
 
 
 def shift_pair(first, final, axis):
@@ -168,19 +289,6 @@
     up = [(i, i + 1) for i in range(count - 1)]
     down = [(i + 1, i) for i in range(count - 1)]
     return lax.ppermute(final, axis, up), lax.ppermute(first, axis, down)
-
-
-def total(value):
-    for axis in ("row", "col"):
-        count = lax.axis_size(axis)
-        if count & (count - 1):
-            value = lax.psum(value, axis)
-            continue
-        hop = 1
-        while hop < count:
-            value = value + lax.ppermute(value, axis, [(i, i ^ hop) for i in range(count)])
-            hop *= 2
-    return value
 
 
 def body(rows, weights, pool, desired, plan, beam_ref, step_size, smoothing, active):
@@ -231,12 +339,7 @@
         name="moments",
     )(weights, pool, pool, pool, xt, xb, xe)
 
-    left, right = shift_pair(first, final, "col")
-    halo = jnp.concatenate([left, right], axis=1)
-    top, bottom = shift_pair(halo[:1], halo[-1:], "row")
-    halo = jnp.concatenate([top, halo, bottom], axis=0)
-
-    sums = total(sums)
+    sums, halo = share(sums, first, final)
     gram, lapped, cross = sums[:beams, :count], sums[:beams, count : 2 * count], sums[beams : beams + count, :count]
     refs = desired.shape[1]
     pick = (beam_ref[:, None] == jnp.arange(refs, dtype=jnp.int32)[None, :]).astype(F32)
@@ -253,11 +356,6 @@
     c1 = live[1] * rate * jnp.dot(error1, chosen[1].T, precision=high)
 
     mix = jnp.concatenate([c0 + c1, s1 * c0], axis=1)
-    mix = (mix[:, None, :, None] * jnp.eye(8, dtype=F32)[None, :, None, :]).reshape(beams * 8, 2 * count * 8)
-    mix_hi = lax.reduce_precision(mix, 8, 7)
-    mix_lo = (mix - mix_hi).astype(BF16)
-    mix_hi = mix_hi.astype(BF16)
-    mix = jnp.concatenate([mix_hi, mix_hi, mix_lo], axis=1)
     flags = jnp.stack([row_i > 0, row_i < row_n - 1, col_i > 0, col_i < col_n - 1]).astype(F32)
 
     smem = pl.BlockSpec(memory_space=pltpu.SMEM)
@@ -266,10 +364,16 @@
         grid=(blocks,),
         in_specs=[smem, smem, smem, block(beams), previous(beams), following(beams), whole(beams, 8, cols),
                   whole(beams, 8, cols), whole(blocks + 2, 4, beams * rows), block(count), block(count),
-                  whole(beams * 8, 6 * count * 8)],
+                  whole(beams, 2 * count)],
         out_specs=block(beams),
         out_shape=jax.ShapeDtypeStruct(weights.shape, F32),
-        scratch_shapes=[pltpu.VMEM((3, beams, rows, 128), F32), pltpu.VMEM((rows + 16, cols + 128), F32)],
+        scratch_shapes=[
+            pltpu.VMEM((3, beams, rows, 128), F32),
+            pltpu.VMEM((2, rows + 8, 128), F32),
+            pltpu.VMEM((beams * 8, 6 * count * 8), BF16),
+            pltpu.VMEM((cols // 128 + 1, rows + 16, 128), F32),
+            pltpu.VMEM((cols // 128 + 1, rows + 8, 128), F32),
+        ],
         compiler_params=pltpu.CompilerParams(vmem_limit_bytes=LIMIT),
         cost_estimate=pl.CostEstimate(flops=10**10, bytes_accessed=10**8, transcendentals=0),
         name="update",
@@ -280,4 +384,4 @@
 def solution(mesh):
     in_specs = (P(None, "row", "col"), P(None, "row", "col"), P(), P(), P(), P(), P(), P())
     out_specs = (P(None, "row", "col"), P())
-    return jax.shard_map(functools.partial(body, 32), mesh=mesh, in_specs=in_specs, out_specs=out_specs, check_vma=False)
+    return jax.shard_map(functools.partial(body, 64), mesh=mesh, in_specs=in_specs, out_specs=out_specs, check_vma=False)

time: 275 us -> 219 us (0.80)
  Pallas kernels: 191 us -> 169 us
  starting transfers between devices: 39.4 us -> 17.4 us
  waiting for transfers between devices: 7.02 us -> 0.02 us
  other arithmetic: 11.3 us -> 7.77 us
  local copies, waits for them, and re-layouts: 20.3 us -> 17.3 us
    pallas_call x1, Pallas kernels: 150 us -> 105 us  [body(): pl.pallas_call(update_kernel, grid=(blocks,), in_specs=[smem, smem, smem,...]
    pallas_call x0 -> x1, Pallas kernels: none -> 24.1 us  [share(): pl.pallas_call(functools.partial(share_kernel, row_n, col_n), in_specs=[v...]
    ppermute x10 -> x6, starting transfers between devices: 31.2 us -> 17.4 us  [shift_pair(): return (lax.ppermute(final, axis, up), lax.ppermute(first, axis, down))]
    ppermute x5 -> x0, starting transfers between devices: 8.23 us -> none  [total(): lax.ppermute(value, axis, [(i, i ^ hop) for i in range(count)])]
    ppermute x5 -> x0, waiting for transfers between devices: 4.44 us -> none  [total(): lax.ppermute(value, axis, [(i, i ^ hop) for i in range(count)])]
    mul x2 -> x0, local copies, waits for them, and re-layouts: 2.85 us -> none  [body(): mix[:, None, :, None] * jnp.eye(8, dtype=F32)[None, :, None, :]]
    unnamed x22 -> x18, local copies, waits for them, and re-layouts: 7.57 us -> 7.6 us
  transfers between devices with their start and end apart: 15 -> 6, of which waited for: 5 -> 0; matrix products, arithmetic and copies ran while one was open for 11% -> 11% of each run, Pallas kernels for 15% -> 30%
where the time goes in v2:
time: 219 us; the launch traced here: 216 us
  Pallas kernels  169 us (77%)
  starting transfers between devices  17.4 us (8%)
  local copies, waits for them, and re-layouts  17.3 us (8%)
  other arithmetic  7.77 us (4%)
  matrix products  3.36 us (2%)
    pallas_call x1, Pallas kernels, body(): pl.pallas_call(update_kernel, grid=(blocks,), in_specs=[smem, smem, smem,...  105 us
    pallas_call x1, Pallas kernels, body(): pl.pallas_call(moments_kernel, grid=(blocks,), in_specs=[block(beams), bl...  40.2 us
    pallas_call x1, Pallas kernels, share(): pl.pallas_call(functools.partial(share_kernel, row_n, col_n), in_specs=[v...  24.1 us
    ppermute x6, starting transfers between devices, shift_pair(): return (lax.ppermute(final, axis, up), lax.ppermute(first, axis, down))  17.4 us
    unnamed x18, local copies, waits for them, and re-layouts  7.6 us
    slice x1, local copies, waits for them, and re-layouts, body(): xl, xr = shift_pair(pool[:, :, 0], pool[:, :, -1], 'col')  5.47 us
  transfers between devices with their start and end apart: 6, of which 0 were waited for; matrix products, arithmetic and copies ran while one was open for 11% of the time, Pallas kernels for 30%

profile of v2, /device:TPU:1, one launch (start us, length us, event | category | flops | bytes accessed | tf_op | source)
XLA Modules:
  0.0 216.2 jit_solution(8719859131457213125)
XLA Ops:
  0.6 0.0 copy-start
  0.6 1.8 fusion.20
  2.4 2.0 collective-permute-start.3
  4.4 4.5 %collective-permute-start.2 = (f32[12,8,512]{2,1,0:T(8,128)}, f32[12,8,512]{2,1,0:T(8,128)S(1)}, u32[]{:S(2)}, u32[]{:S(2)}) collective-permute-start(f32[12,8,512]{2,1,0:T(8,128)} %get-tuple-element.22), channel_id=1, source_target_pairs={{0,8},{8,16},{16,24},{1,9},{9,17},{17,25},{2,10},{10,18},{18,26},{... | collective-permute-start | bytes 589832 | tf_op jit(solution)/shard_map/ppermute | solution.py:291
  8.9 2.4 %fusion.18 = (f32[40,8,512]{2,1,0:T(8,128)}, f32[40,8,512]{2,1,0:T(8,128)}) fusion(f32[40,512,512]{2,1,0:T(8,128)} %wn_ref.1), kind=kLoop, calls=%fused_computation.37 | loop fusion | bytes 2621440 | tf_op jit(solution)/shard_map/slice | solution.py:308
  11.3 1.9 collective-permute-start.1
  13.3 5.5 %fusion.19 = (f32[12,512,1]{2,1,0:T(8,128)S(1)}, f32[12,512,1]{2,1,0:T(8,128)}) fusion(f32[12,512,512]{2,1,0:T(8,128)} %x_ref.3), kind=kLoop, calls=%fused_computation.38 | loop fusion | bytes 98304 | tf_op jit(solution)/shard_map/slice | solution.py:305
  18.7 0.0 copy-start.5
  18.7 0.0 copy-start.6
  18.7 0.0 copy-start.7
  18.7 3.3 %copy.33 = f32[12,512,1]{1,0,2:T(8,128)} copy(f32[12,512,1]{2,1,0:T(8,128)} %get-tuple-element.20) | data formatting | bytes 49152
  22.0 3.7 %collective-permute-start.5 = (f32[12,512]{1,0:T(8,128)}, f32[12,512]{1,0:T(8,128)}, u32[]{:S(2)}, u32[]{:S(2)}) collective-permute-start(f32[12,512]{1,0:T(8,128)} %bitcast.18), channel_id=1, source_target_pairs={{0,1},{1,2},{2,3},{3,4},{4,5},{5,6},{6,7},{8,9},{9,10},{10,11},{11... | collective-permute-start | bytes 73736 | tf_op jit(solution)/shard_map/ppermute | solution.py:291
  25.7 2.1 copy.32
  27.8 1.3 collective-permute-start.4
  29.1 0.0 copy-done.5
  29.2 0.0 copy-done
  29.2 0.9 fusion.6
  30.0 0.0 copy-done.6
  30.0 0.0 copy-done.7
  30.1 1.2 compare_select_fusion
  31.3 0.7 add_convert_fusion.flag_ref
  31.9 0.5 add.13.a_ref
  32.4 0.0 collective-permute-done.5
  32.4 4.1 %collective-permute-start = (f32[40,8,512]{2,1,0:T(8,128)}, f32[40,8,512]{2,1,0:T(8,128)S(1)}, u32[]{:S(2)}, u32[]{:S(2)}) collective-permute-start(f32[40,8,512]{2,1,0:T(8,128)} %get-tuple-element.18), channel_id=1, source_target_pairs={{0,8},{8,16},{16,24},{1,9},{9,17},{17,25},{2,10},{10,18},{18,26},{... | collective-permute-start | bytes 1966088 | tf_op jit(solution)/shard_map/ppermute | solution.py:291
  36.5 0.0 collective-permute-done.4
  36.5 4.1 %select_select_fusion.xe_ref = f32[12,512,128]{2,1,0:T(8,128)} fusion(f32[12,512]{1,0:T(8,128)} %collective-permute-done.5, f32[12,512]{1,0:T(8,128)S(1)} %collective-permute-done.4, pred[128]{0:T(512)(128)(4,1)S(1)} %get-tuple-element.32, pred[128]{0:T(512)(128)(4,1)S(1)} %get-tuple-element.33), kind=kLoop, calls=%fused_computation | loop fusion | flops 1572864 | bytes 3195136 | tf_op jit(solution)/shard_map/jit(_where)/select_n | solution.py:307
  40.6 0.0 collective-permute-done.3.xb_ref
  40.6 0.0 copy-start.3
  40.6 0.0 collective-permute-done.2.xt_ref
  40.6 0.7 copy-done.3
  41.3 0.0 copy-start.4
  41.3 0.7 copy-done.4
  42.0 40.2 %moments.1 = (f32[56,128]{1,0:T(8,128)}, f32[12,512,512]{2,1,0:T(8,128)}, f32[8,2,2560]{2,1,0:T(2,128)}, f32[8,2,2560]{2,1,0:T(2,128)}) custom-call(f32[40,512,512]{2,1,0:T(8,128)} %wn_ref.1, f32[12,512,512]{2,1,0:T(8,128)} %x_ref.3, f32[12,512,512]{2,1,0:T(8,128)} %x_ref.3, f32[12,512,512]{2,1,0:T(8,128)} %x_ref.3, f32[12,8,512]{2,1,0:T(8,128)} %copy-done.4, ...), custom_call_target="tpu_custom_call" | custom-call | flops 10000000000 | bytes 100000000 | tf_op jit(solution)/shard_map/moments/pallas_call | solution.py:324
  82.2 24.1 %share.1 = (f32[56,128]{1,0:T(8,128)}, f32[10,4,2560]{2,1,0:T(4,128)}) custom-call(f32[56,128]{1,0:T(8,128)} %get-tuple-element.8.sums_ref, f32[8,2,2560]{2,1,0:T(2,128)} %get-tuple-element.9.first_ref, f32[8,2,2560]{2,1,0:T(2,128)} %get-tuple-element.10.final_ref), custom_call_target="tpu_custom_call" | custom-call | flops 1000000 | bytes 10000000 | tf_op jit(solution)/shard_map/share/pallas_call | solution.py:263
  106.3 0.9 fusion.3
  107.2 0.2 broadcast_multiply_fusion
  107.5 1.0 fusion.2
  108.4 0.2 fusion.10
  108.6 0.6 pad_maximum_fusion.1
  109.2 0.2 fusion
  109.5 0.7 pad_maximum_fusion.coef_ref
  110.1 0.0 collective-permute-done.1.wb_ref
  110.1 0.0 collective-permute-done.wt_ref
  110.1 0.0 copy-start.2
  110.1 0.8 copy-done.2
  111.0 0.0 copy-start.1
  111.0 105.0 %update.1 = f32[40,512,512]{2,1,0:T(8,128)} custom-call(f32[40]{0:T(128)} %add.13.a_ref, f32[40]{0:T(128)} %get-tuple-element.27.b_ref, f32[4]{0:T(128)} %add_convert_fusion.flag_ref, f32[40,512,512]{2,1,0:T(8,128)} %wn_ref.1, f32[40,512,512]{2,1,0:T(8,128)} %wn_ref.1, f32[40,512,512]{2,1,0:T(8,128)} %wn_ref.1, f32[40,8,512]{2,1,0:T(8,128)} %copy-done.2, ...), custom_call_target="tpu_custom_call" | custom-call | flops 10000000000 | bytes 100000000 | tf_op jit(solution)/shard_map/update/pallas_call | solution.py:362
  216.0 0.0 copy-done.1
  (2 shorter events, 0.0 us)
Async XLA Ops:
  0.6 28.5 %copy-start = (f32[12,8]{0,1:T(8,128)S(1)}, f32[12,8]{0,1:T(8,128)}, u32[]{:S(2)}) copy-start(f32[12,8]{0,1:T(8,128)} %param.10) | copy-start | bytes 1156
  2.4 38.2 %collective-permute-start.3 = (f32[12,8,512]{2,1,0:T(8,128)}, f32[12,8,512]{2,1,0:T(8,128)S(1)}, u32[]{:S(2)}, u32[]{:S(2)}) collective-permute-start(f32[12,8,512]{2,1,0:T(8,128)} %get-tuple-element.21), channel_id=1, source_target_pairs={{8,0},{16,8},{24,16},{9,1},{17,9},{25,17},{10,2},{18,10},{26,18},{... | collective-permute-start | bytes 589832 | tf_op jit(solution)/shard_map/ppermute | solution.py:291
  4.4 36.2 %collective-permute-start.2 = (f32[12,8,512]{2,1,0:T(8,128)}, f32[12,8,512]{2,1,0:T(8,128)S(1)}, u32[]{:S(2)}, u32[]{:S(2)}) collective-permute-start(f32[12,8,512]{2,1,0:T(8,128)} %get-tuple-element.22), channel_id=1, source_target_pairs={{0,8},{8,16},{16,24},{1,9},{9,17},{17,25},{2,10},{10,18},{18,26},{... | collective-permute-start | bytes 589832 | tf_op jit(solution)/shard_map/ppermute | solution.py:291
  11.3 98.8 %collective-permute-start.1 = (f32[40,8,512]{2,1,0:T(8,128)}, f32[40,8,512]{2,1,0:T(8,128)}, u32[]{:S(2)}, u32[]{:S(2)}) collective-permute-start(f32[40,8,512]{2,1,0:T(8,128)} %get-tuple-element.17), channel_id=1, source_target_pairs={{8,0},{16,8},{24,16},{9,1},{17,9},{25,17},{10,2},{18,10},{26,18},{... | collective-permute-start | bytes 1966088 | tf_op jit(solution)/shard_map/ppermute | solution.py:291
  18.7 10.4 %copy-start.5 = (s32[2,16]{1,0:T(2,128)S(1)}, s32[2,16]{1,0:T(2,128)}, u32[]{:S(2)}) copy-start(s32[2,16]{1,0:T(2,128)} %param.11) | copy-start | bytes 388
  18.7 11.3 %copy-start.6 = (s32[40]{0:T(128)S(1)}, s32[40]{0:T(128)}, u32[]{:S(2)}) copy-start(s32[40]{0:T(128)} %param.15) | copy-start | bytes 484
  18.7 11.3 %copy-start.7 = (f32[40]{0:T(128)S(1)}, f32[40]{0:T(128)}, u32[]{:S(2)}) copy-start(f32[40]{0:T(128)} %param.13) | copy-start | bytes 484
  22.0 10.4 %collective-permute-start.5 = (f32[12,512]{1,0:T(8,128)}, f32[12,512]{1,0:T(8,128)}, u32[]{:S(2)}, u32[]{:S(2)}) collective-permute-start(f32[12,512]{1,0:T(8,128)} %bitcast.18), channel_id=1, source_target_pairs={{0,1},{1,2},{2,3},{3,4},{4,5},{5,6},{6,7},{8,9},{9,10},{10,11},{11... | collective-permute-start | bytes 73736 | tf_op jit(solution)/shard_map/ppermute | solution.py:291
  27.8 8.7 %collective-permute-start.4 = (f32[12,512]{1,0:T(8,128)}, f32[12,512]{1,0:T(8,128)S(1)}, u32[]{:S(2)}, u32[]{:S(2)}) collective-permute-start(f32[12,512]{1,0:T(8,128)} %bitcast.17), channel_id=1, source_target_pairs={{1,0},{2,1},{3,2},{4,3},{5,4},{6,5},{7,6},{9,8},{10,9},{11,10},{12... | collective-permute-start | bytes 73736 | tf_op jit(solution)/shard_map/ppermute | solution.py:291
  32.4 77.7 %collective-permute-start = (f32[40,8,512]{2,1,0:T(8,128)}, f32[40,8,512]{2,1,0:T(8,128)S(1)}, u32[]{:S(2)}, u32[]{:S(2)}) collective-permute-start(f32[40,8,512]{2,1,0:T(8,128)} %get-tuple-element.18), channel_id=1, source_target_pairs={{0,8},{8,16},{16,24},{1,9},{9,17},{17,25},{2,10},{10,18},{18,26},{... | collective-permute-start | bytes 1966088 | tf_op jit(solution)/shard_map/ppermute | solution.py:291
  40.6 0.7 copy-start.3
  41.3 0.7 copy-start.4
  110.1 0.8 copy-start.2
  111.0 105.0 %copy-start.1 = (f32[12,8]{0,1:T(8,128)S(1)}, f32[12,8]{0,1:T(8,128)}, u32[]{:S(2)}) copy-start(f32[12,8]{0,1:T(8,128)} %param.10) | copy-start | bytes 1156

commit v3 on v2

--- a/solution.py
+++ b/solution.py
@@ -29,6 +29,113 @@
     r = lax.broadcasted_iota(jnp.int32, (rows, cols), 0)
     c = lax.broadcasted_iota(jnp.int32, (rows, cols), 1)
     return jnp.where(hit(r, c), 1.0, 0.0).astype(F32)
+
+
+def edge(tile, lane):
+    pick = one_hot(8, 128, lambda r, c: c == r + lane).astype(BF16)
+    h, m = split(tile)
+    l = (tile - h.astype(F32) - m.astype(F32)).astype(BF16)
+    return (
+        lax.dot_general(pick, h, NT, preferred_element_type=F32)
+        + lax.dot_general(pick, m, NT, preferred_element_type=F32)
+        + lax.dot_general(pick, l, NT, preferred_element_type=F32)
+    )[:2]
+
+
+def widen(raw):
+    h = raw.astype(BF16).astype(F32)
+    m = (raw - h).astype(BF16).astype(F32)
+    l = raw - h - m
+    stack = jnp.concatenate([h, m, l, jnp.zeros_like(h)], axis=0)
+    r = lax.broadcasted_iota(jnp.int32, (16, 128), 0)
+    c = lax.broadcasted_iota(jnp.int32, (16, 128), 1)
+    k = r % 4
+    spot = jnp.where(k < 2, k + 126, k - 2)
+    place = jnp.where((c == spot) & (r < 12), 1.0, 0.0).astype(BF16)
+    return jnp.dot(stack.T.astype(BF16), place, preferred_element_type=F32)
+
+
+def remote(src, dst, s, r, device):
+    return pltpu.make_async_remote_copy(
+        src_ref=src, dst_ref=dst, send_sem=s, recv_sem=r, device_id=device,
+        device_id_type=pl.DeviceIdType.MESH,
+    )
+
+
+def greet(others):
+    barrier = pltpu.get_barrier_semaphore()
+    for other in others:
+        pl.semaphore_signal(barrier, inc=1, device_id=other, device_id_type=pl.DeviceIdType.MESH)
+    pl.semaphore_wait(barrier, len(others))
+
+
+def around(row, col, row_n, col_n):
+    right = (row, lax.rem(col + 1, col_n))
+    left = (row, lax.rem(col + col_n - 1, col_n))
+    below = (lax.rem(row + 1, row_n), col)
+    above = (lax.rem(row + row_n - 1, row_n), col)
+    return right, left, below, above
+
+
+def pool_kernel(
+    row_n, col_n, x_ref, xt_ref, xb_ref, xe_ref,
+    near, far, first, final, left_in, right_in, top_in, bottom_in, local, send, recv
+):
+    row, col = lax.axis_index("row"), lax.axis_index("col")
+    pool, height, cols = x_ref.shape
+    right, left, below, above = around(row, col, row_n, col_n)
+    get_near = pltpu.make_async_copy(x_ref.at[:, :, pl.ds(0, 128)], near, local.at[0])
+    get_far = pltpu.make_async_copy(x_ref.at[:, :, pl.ds(cols - 128, 128)], far, local.at[1])
+    get_near.start()
+    get_far.start()
+    greet([right, left, below, above])
+    down = remote(x_ref.at[:, pl.ds(height - 8, 8)], top_in, send.at[0], recv.at[0], below)
+    up = remote(x_ref.at[:, pl.ds(0, 8)], bottom_in, send.at[1], recv.at[1], above)
+    down.start()
+    up.start()
+    get_near.wait()
+    first[...] = edge(near[...].reshape(pool * height, 128), 0)
+    to_left = remote(first, right_in, send.at[2], recv.at[2], left)
+    to_left.start()
+    get_far.wait()
+    final[...] = edge(far[...].reshape(pool * height, 128), 126)
+    to_right = remote(final, left_in, send.at[3], recv.at[3], right)
+    to_right.start()
+    down.wait()
+    up.wait()
+    xt_ref[...] = jnp.where(row > 0, top_in[...], 0.0)
+    xb_ref[...] = jnp.where(row < row_n - 1, bottom_in[...], 0.0)
+    to_left.wait()
+    to_right.wait()
+    before = jnp.where(col > 0, left_in[...], 0.0)
+    after = jnp.where(col < col_n - 1, right_in[...], 0.0)
+    xe_ref[...] = widen(jnp.concatenate([before, after], axis=0)).reshape(xe_ref.shape)
+
+
+def pool_halos(pool):
+    row_n, col_n = lax.axis_size("row"), lax.axis_size("col")
+    count, height, cols = pool.shape
+    vmem = pl.BlockSpec(memory_space=pltpu.VMEM)
+    strip = pltpu.VMEM((count, height, 128), F32)
+    line = pltpu.VMEM((2, count * height), F32)
+    slab = pltpu.VMEM((count, 8, cols), F32)
+    return pl.pallas_call(
+        functools.partial(pool_kernel, row_n, col_n),
+        in_specs=[pl.BlockSpec(memory_space=pl.ANY)],
+        out_specs=[vmem] * 3,
+        out_shape=[
+            jax.ShapeDtypeStruct((count, 8, cols), F32),
+            jax.ShapeDtypeStruct((count, 8, cols), F32),
+            jax.ShapeDtypeStruct((count, height, 128), F32),
+        ],
+        scratch_shapes=[
+            strip, strip, line, line, line, line, slab, slab,
+            pltpu.SemaphoreType.DMA((2,)), pltpu.SemaphoreType.DMA((4,)), pltpu.SemaphoreType.DMA((4,)),
+        ],
+        compiler_params=pltpu.CompilerParams(collective_id=1, has_side_effects=True, vmem_limit_bytes=LIMIT),
+        cost_estimate=pl.CostEstimate(flops=10**6, bytes_accessed=10**7, transcendentals=0),
+        name="pool_halos",
+    )(pool)
 
 
 def moments_kernel(w_ref, x_ref, xp_ref, xn_ref, xt_ref, xb_ref, xe_ref, out_ref, lx_ref, el_ref, er_ref, acc_ref):
@@ -59,16 +166,6 @@
         right = jnp.concatenate([rh, rh, rl], axis=1)
         acc_ref[...] += lax.dot_general(left, right, NT, preferred_element_type=F32)
 
-    def edge(tile, lane):
-        pick = one_hot(8, 128, lambda r, c: c == r + lane).astype(BF16)
-        h, m = split(tile)
-        l = (tile - h.astype(F32) - m.astype(F32)).astype(BF16)
-        return (
-            lax.dot_general(pick, h, NT, preferred_element_type=F32)
-            + lax.dot_general(pick, m, NT, preferred_element_type=F32)
-            + lax.dot_general(pick, l, NT, preferred_element_type=F32)
-        )[:2]
-
     el_ref[0] = edge(w_ref[:, :, :128].reshape(beams * rows, 128), 0)
     er_ref[0] = edge(w_ref[:, :, cols - 128 :].reshape(beams * rows, 128), 126)
 
@@ -92,17 +189,7 @@
     tiles = cols // 128
 
     def make_tile(j):
-        raw = halo_ref[j]
-        h = raw.astype(BF16).astype(F32)
-        m = (raw - h).astype(BF16).astype(F32)
-        l = raw - h - m
-        stack = jnp.concatenate([h, m, l, jnp.zeros_like(h)], axis=0)
-        r = lax.broadcasted_iota(jnp.int32, (16, 128), 0)
-        c = lax.broadcasted_iota(jnp.int32, (16, 128), 1)
-        k = r % 4
-        spot = jnp.where(k < 2, k + 126, k - 2)
-        place = jnp.where((c == spot) & (r < 12), 1.0, 0.0).astype(BF16)
-        tile = jnp.dot(stack.T.astype(BF16), place, preferred_element_type=F32)
+        tile = widen(halo_ref[j])
         tile_ref[j % 3] = tile.reshape(beams, rows, 128)
 
     @pl.when(i == 0)
@@ -160,9 +247,9 @@
         a, b = a_ref[n], b_ref[n]
         for k in range(tiles):
             lanes = pl.ds(128 * k, 128)
-            s_ref[k, pl.ds(0, 8)] = jnp.where(i == 0, wt_ref[n, :, lanes], wp_ref[n, :, lanes])
+            s_ref[k, pl.ds(0, 8)] = jnp.where(i == 0, wt_ref[n, :, lanes] * flag_ref[0], wp_ref[n, :, lanes])
             s_ref[k, pl.ds(8, rows)] = w_ref[n, :, lanes]
-            s_ref[k, pl.ds(rows + 8, 8)] = jnp.where(i == last, wb_ref[n, :, lanes], wn_ref[n, :, lanes])
+            s_ref[k, pl.ds(rows + 8, 8)] = jnp.where(i == last, wb_ref[n, :, lanes] * flag_ref[1], wn_ref[n, :, lanes])
         s_ref[tiles, pl.ds(0, 8)] = tile_ref[before, n, pl.ds(rows - 8, 8)]
         s_ref[tiles, pl.ds(8, rows)] = tile_ref[here, n]
         s_ref[tiles, pl.ds(rows + 8, 8)] = tile_ref[after, n, pl.ds(0, 8)]
@@ -194,50 +281,42 @@
 
 
 def share_kernel(
-    row_n, col_n, sums_ref, first_ref, final_ref, out_ref, halo_ref,
-    held, got, left_in, right_in, corner_up, corner_down, corner_top, corner_bottom,
+    row_n, col_n, w_ref, sums_ref, first_ref, final_ref, wt_ref, wb_ref, out_ref, halo_ref,
+    row_got, col_got, part, left_in, right_in, corner_up, corner_down, corner_top, corner_bottom,
     send, recv, edge_send, edge_recv
 ):
     row, col = lax.axis_index("row"), lax.axis_index("col")
     blocks = first_ref.shape[0]
-
-    def partner(me, hop):
-        return me + hop - 2 * hop * lax.rem(lax.div(me, hop), 2)
-
-    hops = []
-    for hop in [1 << k for k in range(row_n.bit_length() - 1)]:
-        hops.append((partner(row, hop), col))
-    for hop in [1 << k for k in range(col_n.bit_length() - 1)]:
-        hops.append((row, partner(col, hop)))
-    right = (row, lax.rem(col + 1, col_n))
-    left = (row, lax.rem(col + col_n - 1, col_n))
-    below = (lax.rem(row + 1, row_n), col)
-    above = (lax.rem(row + row_n - 1, row_n), col)
-
-    barrier = pltpu.get_barrier_semaphore()
-    others = hops + [right, left, below, above]
-    for other in others:
-        pl.semaphore_signal(barrier, inc=1, device_id=other, device_id_type=pl.DeviceIdType.MESH)
-    pl.semaphore_wait(barrier, len(others))
-
-    def copy(src, dst, s, r, device):
-        return pltpu.make_async_remote_copy(
-            src_ref=src, dst_ref=dst, send_sem=s, recv_sem=r, device_id=device,
-            device_id_type=pl.DeviceIdType.MESH,
-        )
-
-    to_right = copy(final_ref, left_in, edge_send.at[0], edge_recv.at[0], right)
-    to_left = copy(first_ref, right_in, edge_send.at[1], edge_recv.at[1], left)
-    held[0] = sums_ref[...]
-    for k, other in enumerate(hops):
-        move = copy(held.at[k], got.at[k], send.at[k], recv.at[k], other)
+    height = w_ref.shape[1]
+    right, left, below, above = around(row, col, row_n, col_n)
+    row_peers = [(lax.rem(row + d, row_n), col) for d in range(1, row_n)]
+    col_peers = [(row, lax.rem(col + d, col_n)) for d in range(1, col_n)]
+    greet(row_peers + col_peers)
+
+    gather = [
+        remote(sums_ref, row_got.at[row], send.at[k], recv.at[k], peer) for k, peer in enumerate(row_peers)
+    ]
+    to_right = remote(final_ref, left_in, edge_send.at[0], edge_recv.at[0], right)
+    to_left = remote(first_ref, right_in, edge_send.at[1], edge_recv.at[1], left)
+    w_down = remote(w_ref.at[:, pl.ds(height - 8, 8)], wt_ref, edge_send.at[4], edge_recv.at[4], below)
+    w_up = remote(w_ref.at[:, pl.ds(0, 8)], wb_ref, edge_send.at[5], edge_recv.at[5], above)
+    for move in gather + [to_right, to_left, w_down, w_up]:
         move.start()
-        if k == 0:
-            to_right.start()
-            to_left.start()
+    row_got[row] = sums_ref[...]
+    for move in gather:
         move.wait()
-        held[k + 1] = held[k] + got[k]
-    out_ref[...] = held[len(hops)]
+    value = row_got[0]
+    for k in range(1, row_n):
+        value = value + row_got[k]
+    part[...] = value
+    base = row_n - 1
+    spread = [
+        remote(part, col_got.at[col], send.at[base + k], recv.at[base + k], peer)
+        for k, peer in enumerate(col_peers)
+    ]
+    for move in spread:
+        move.start()
+    col_got[col] = value
 
     to_right.wait()
     to_left.wait()
@@ -245,50 +324,60 @@
     halo_ref[pl.ds(1, blocks), pl.ds(2, 2)] = jnp.where(col < col_n - 1, right_in[...], 0.0)
     corner_up[...] = halo_ref[1]
     corner_down[...] = halo_ref[blocks]
-    down = copy(corner_down, corner_top, edge_send.at[2], edge_recv.at[2], below)
-    up = copy(corner_up, corner_bottom, edge_send.at[3], edge_recv.at[3], above)
+    down = remote(corner_down, corner_top, edge_send.at[2], edge_recv.at[2], below)
+    up = remote(corner_up, corner_bottom, edge_send.at[3], edge_recv.at[3], above)
     down.start()
     up.start()
+
+    for move in spread:
+        move.wait()
+    value = col_got[0]
+    for k in range(1, col_n):
+        value = value + col_got[k]
+    out_ref[...] = value
     down.wait()
     up.wait()
     halo_ref[0] = jnp.where(row > 0, corner_top[...], 0.0)
     halo_ref[blocks + 1] = jnp.where(row < row_n - 1, corner_bottom[...], 0.0)
-
-
-def share(sums, first, final):
+    w_down.wait()
+    w_up.wait()
+
+
+def share(weights, sums, first, final):
     row_n, col_n = lax.axis_size("row"), lax.axis_size("col")
+    beams, _, cols = weights.shape
     blocks, _, length = first.shape
-    hops = row_n.bit_length() + col_n.bit_length() - 2
+    moves = row_n + col_n - 2
     vmem = pl.BlockSpec(memory_space=pltpu.VMEM)
+    hbm = pl.BlockSpec(memory_space=pl.ANY)
+    slab = jax.ShapeDtypeStruct((beams, 8, cols), F32)
     return pl.pallas_call(
         functools.partial(share_kernel, row_n, col_n),
-        in_specs=[vmem] * 3,
-        out_specs=[vmem] * 2,
-        out_shape=[jax.ShapeDtypeStruct(sums.shape, F32), jax.ShapeDtypeStruct((blocks + 2, 4, length), F32)],
+        in_specs=[hbm] + [vmem] * 3,
+        out_specs=[hbm, hbm, vmem, vmem],
+        out_shape=[
+            slab, slab,
+            jax.ShapeDtypeStruct(sums.shape, F32),
+            jax.ShapeDtypeStruct((blocks + 2, 4, length), F32),
+        ],
         scratch_shapes=[
-            pltpu.VMEM((hops + 1, *sums.shape), F32),
-            pltpu.VMEM((hops, *sums.shape), F32),
+            pltpu.VMEM((row_n, *sums.shape), F32),
+            pltpu.VMEM((col_n, *sums.shape), F32),
+            pltpu.VMEM(sums.shape, F32),
             pltpu.VMEM(first.shape, F32),
             pltpu.VMEM(first.shape, F32),
             *[pltpu.VMEM((4, length), F32) for _ in range(4)],
-            pltpu.SemaphoreType.DMA((hops,)),
-            pltpu.SemaphoreType.DMA((hops,)),
-            pltpu.SemaphoreType.DMA((4,)),
-            pltpu.SemaphoreType.DMA((4,)),
+            pltpu.SemaphoreType.DMA((moves,)),
+            pltpu.SemaphoreType.DMA((moves,)),
+            pltpu.SemaphoreType.DMA((6,)),
+            pltpu.SemaphoreType.DMA((6,)),
         ],
         compiler_params=pltpu.CompilerParams(
             collective_id=0, has_side_effects=True, vmem_limit_bytes=LIMIT
         ),
         cost_estimate=pl.CostEstimate(flops=10**6, bytes_accessed=10**7, transcendentals=0),
         name="share",
-    )(sums, first, final)
-
-
-def shift_pair(first, final, axis):
-    count = lax.axis_size(axis)
-    up = [(i, i + 1) for i in range(count - 1)]
-    down = [(i + 1, i) for i in range(count - 1)]
-    return lax.ppermute(final, axis, up), lax.ppermute(first, axis, down)
+    )(weights, sums, first, final)
 
 
 def body(rows, weights, pool, desired, plan, beam_ref, step_size, smoothing, active):
@@ -301,11 +390,7 @@
     scale = 1.0 / math.sqrt(height * row_n * cols * col_n)
     high = lax.Precision.HIGHEST
 
-    xt, xb = shift_pair(pool[:, :8], pool[:, -8:], "row")
-    xl, xr = shift_pair(pool[:, :, 0], pool[:, :, -1], "col")
-    lane = jnp.arange(128)[None, None, :]
-    xe = jnp.where(lane == 0, xr[:, :, None], jnp.where(lane == 127, xl[:, :, None], 0.0))
-    wt, wb = shift_pair(weights[:, :8], weights[:, -8:], "row")
+    xt, xb, xe = pool_halos(pool)
 
     def block(n, r=rows, w=cols):
         return pl.BlockSpec((n, r, w), lambda i: (0, i, 0))
@@ -339,7 +424,7 @@
         name="moments",
     )(weights, pool, pool, pool, xt, xb, xe)
 
-    sums, halo = share(sums, first, final)
+    wt, wb, sums, halo = share(weights, sums, first, final)
     gram, lapped, cross = sums[:beams, :count], sums[:beams, count : 2 * count], sums[beams : beams + count, :count]
     refs = desired.shape[1]
     pick = (beam_ref[:, None] == jnp.arange(refs, dtype=jnp.int32)[None, :]).astype(F32)

time: 219 us -> 192 us (0.88)
  starting transfers between devices: 17.4 us -> 0 us
  local copies, waits for them, and re-layouts: 17.3 us -> 0.77 us
  Pallas kernels: 169 us -> 182 us
  other arithmetic: 7.77 us -> 3.66 us
    ppermute x6 -> x0, starting transfers between devices: 17.4 us -> none  [shift_pair(): return (lax.ppermute(final, axis, up), lax.ppermute(first, axis, down))]
    pallas_call x1 -> x2, Pallas kernels: 24.1 us -> 35.8 us  [the longest x1 21.3 us: share(): pl.pallas_call(functools.partial(share_kernel, row_n, col_n), in_specs=[h...]
    slice x3 -> x0, local copies, waits for them, and re-layouts: 9.7 us -> none  [the longest x1 5.47 us: body(): xl, xr = shift_pair(pool[:, :, 0], pool[:, :, -1], 'col')]
    unnamed x18 -> x4, local copies, waits for them, and re-layouts: 7.6 us -> 0.02 us
    select_n x1 -> x0, other arithmetic: 4.11 us -> none  [body(): jnp.where(lane == 0, xr[:, :, None], jnp.where(lane == 127, xl[:, :, None...]
  transfers between devices with their start and end apart: 6 -> 0, of which waited for: 0 -> 0; matrix products, arithmetic and copies ran while one was open for 11% -> 0% of each run, Pallas kernels for 30% -> 0%
where the time goes in v3:
time: 192 us; the launch traced here: 191 us
  Pallas kernels  182 us (95%)
  other arithmetic  3.66 us (2%)
  matrix products  3.36 us (2%)
    pallas_call x1, Pallas kernels, body(): pl.pallas_call(update_kernel, grid=(blocks,), in_specs=[smem, smem, smem,...  106 us
    pallas_call x1, Pallas kernels, body(): pl.pallas_call(moments_kernel, grid=(blocks,), in_specs=[block(beams), bl...  40.4 us
    pallas_call x1, Pallas kernels, share(): pl.pallas_call(functools.partial(share_kernel, row_n, col_n), in_specs=[h...  21.3 us
    pallas_call x1, Pallas kernels, pool_halos(): pl.pallas_call(functools.partial(pool_kernel, row_n, col_n), in_specs=[pl...  14.6 us

profile of v3, /device:TPU:1, one launch (start us, length us, event | category | flops | bytes accessed | tf_op | source)
XLA Modules:
  0.0 190.6 jit_solution(16609419136854144617)
XLA Ops:
  0.6 0.0 copy-start
  0.7 0.6 add_convert_fusion.flag_ref
  1.3 0.8 slice_bitcast_fusion
  2.0 1.2 compare_select_fusion
  3.2 0.6 add.13.a_ref
  3.8 0.0 copy-done
  3.8 0.9 fusion.6
  4.6 14.6 %pool_halos.1 = (f32[12,8,512]{2,1,0:T(8,128)}, f32[12,8,512]{2,1,0:T(8,128)}, f32[12,512,128]{2,1,0:T(8,128)}) custom-call(f32[12,512,512]{2,1,0:T(8,128)} %x_ref.5), custom_call_target="tpu_custom_call" | custom-call | flops 1000000 | bytes 10000000 | tf_op jit(solution)/shard_map/pool_halos/pallas_call | solution.py:122
  19.2 40.4 %moments.1 = (f32[56,128]{1,0:T(8,128)}, f32[12,512,512]{2,1,0:T(8,128)}, f32[8,2,2560]{2,1,0:T(2,128)}, f32[8,2,2560]{2,1,0:T(2,128)}) custom-call(f32[40,512,512]{2,1,0:T(8,128)} %wn_ref.1, f32[12,512,512]{2,1,0:T(8,128)} %x_ref.5, f32[12,512,512]{2,1,0:T(8,128)} %x_ref.5, f32[12,512,512]{2,1,0:T(8,128)} %x_ref.5, f32[12,8,512]{2,1,0:T(8,128)} %get-tuple-element.13.xt_ref, ...), custom_call_target="tpu_custom_call" | custom-call | flops 10000000000 | bytes 100000000 | tf_op jit(solution)/shard_map/moments/pallas_call | solution.py:409
  59.6 21.3 %share.1 = (f32[40,8,512]{2,1,0:T(8,128)}, f32[40,8,512]{2,1,0:T(8,128)}, f32[56,128]{1,0:T(8,128)}, f32[10,4,2560]{2,1,0:T(4,128)}) custom-call(f32[40,512,512]{2,1,0:T(8,128)} %wn_ref.1, f32[56,128]{1,0:T(8,128)} %get-tuple-element.16.sums_ref, f32[8,2,2560]{2,1,0:T(2,128)} %get-tuple-element.17.first_ref, f32[8,2,2560]{2,1,0:T(2,128)} %get-tuple-element.18.final_ref), custom_call_target="tpu_custom_call" | custom-call | flops 1000000 | bytes 10000000 | tf_op jit(solution)/shard_map/share/pallas_call | solution.py:354
  80.9 0.9 fusion.3
  81.8 0.2 broadcast_multiply_fusion
  82.0 1.0 fusion.2
  83.0 0.2 fusion.10
  83.2 0.6 pad_maximum_fusion.1
  83.8 0.2 fusion
  84.0 0.7 pad_maximum_fusion.coef_ref
  84.7 0.0 copy-start.1
  84.7 105.7 %update.1 = f32[40,512,512]{2,1,0:T(8,128)} custom-call(f32[40]{0:T(128)} %add.13.a_ref, f32[40]{0:T(128)} %get-tuple-element.31.b_ref, f32[4]{0:T(128)} %add_convert_fusion.flag_ref, f32[40,512,512]{2,1,0:T(8,128)} %wn_ref.1, f32[40,512,512]{2,1,0:T(8,128)} %wn_ref.1, f32[40,512,512]{2,1,0:T(8,128)} %wn_ref.1, f32[40,8,512]{2,1,0:T(8,128)} %get-tuple-element.19.wt_ref, ...), custom_call_target="tpu_custom_call" | custom-call | flops 10000000000 | bytes 100000000 | tf_op jit(solution)/shard_map/update/pallas_call | solution.py:447
  190.4 0.0 copy-done.1
Async XLA Ops:
  0.6 3.1 %copy-start = (f32[12,8]{0,1:T(8,128)S(1)}, f32[12,8]{0,1:T(8,128)}, u32[]{:S(2)}) copy-start(f32[12,8]{0,1:T(8,128)} %param.10) | copy-start | bytes 1156
  84.7 105.7 %copy-start.1 = (f32[12,8]{0,1:T(8,128)S(1)}, f32[12,8]{0,1:T(8,128)}, u32[]{:S(2)}) copy-start(f32[12,8]{0,1:T(8,128)} %param.10) | copy-start | bytes 1156
